TPU v7x, 256 devices: a whole 4x4x8 slice. The times are simulated.
256 devices in a mesh: ctx: 32 (over z, x_hi, core), kvh: 8 (over y, x_lo).
Axes of the slice: x: 4 (x_hi: 2, x_lo: 2; x = x_hi * 2 + x_lo), y: 4, z: 8, core: 2. Of those that a mesh axis runs over, the one named last changes fastest.
Arguments:
- queries: bfloat16 [512, 128, 128], P('ctx', 'kvh'), may hold values from -60 to 60
- cache_keys: bfloat16 [32768, 8, 128], P('ctx', 'kvh'), may hold values from -30 to 30
- cache_values: bfloat16 [32768, 8, 128], P('ctx', 'kvh'), may hold values from -6 to 6
- new_keys: bfloat16 [512, 8, 128], P('ctx', 'kvh'), may hold values from -8 to 8
- new_values: bfloat16 [512, 8, 128], P('ctx', 'kvh'), may hold values from -6 to 6
- fill_rows: int32 [32], P('ctx'), may hold values from 128 to 1024, as said below
- turn_start: int32 [1], replicated, may hold values from 1024 to 4095
- out_weight: bfloat16 [16384, 16384], P('kvh', 'ctx'), may hold values from -0.046875 to 0.046875
Outputs:
- mixed: bfloat16 [512, 16384], P('kvh', 'ctx')
Inputs may be any that keep to these rules, and one draw needn't show every extreme that they name: `fill_rows`: each is a multiple of 128; some shard is full.
All inputs are finite; a program needn't handle non-finite values.
Results may differ from a plain program's by a relative error of at most 0.02.
Values may be sent and summed in bfloat16 or wider, within the bound.
No kernel may reach another device: no remote copies, remote signals or barrier semaphores. Data moves between devices by JAX's collectives and lax.ppermute only.
A program may use at most 64 MiB of HBM per device.

v0:
```python
import functools
import math

import jax
import jax.numpy as jnp
from jax import lax
from jax.experimental import pallas as pl
from jax.experimental.pallas import tpu as pltpu
from jax.sharding import PartitionSpec as P

NEG = -1e30
ROPE_BASE = 500000.0
LOG2E = 1.4426950408889634
HD = 128
STAT = 16
VMEM = pl.BlockSpec(memory_space=pltpu.VMEM)
HBM = pl.BlockSpec(memory_space=pltpu.HBM)


def prepare_kernel(q_hbm, k_hbm, v_hbm, fresh, cosine, sine, q_out, pack_out, q_in, turned, sems):
    n = k_hbm.shape[0]
    piece = n // 4
    copies = [pltpu.make_async_copy(q_hbm, q_in, sems.at[0])]
    for i in range(8):
        source = (k_hbm, v_hbm)[i // 4].at[i % 4 * piece : (i % 4 + 1) * piece]
        target = pack_out.at[i * piece : (i + 1) * piece]
        copies.append(pltpu.make_async_copy(source, target, sems.at[1 + i]))
    for copy in copies:
        copy.start()
    cos, sin = cosine[...], sine[...]
    new_k = fresh[0:16, :].astype(jnp.float32)
    new_k = new_k * cos + pltpu.roll(new_k, HD // 2, 1) * sin
    pack_out[2 * n : 2 * n + 16, :] = new_k.astype(jnp.bfloat16)
    pack_out[2 * n + 16 : 2 * n + NOTE, :] = fresh[16:NOTE, :]
    copies[0].wait()
    tokens, heads, width = q_in.shape
    old = q_in[...].astype(jnp.float32)
    swapped = pltpu.roll(old.reshape(tokens * heads, width), HD // 2, 1).reshape(old.shape)
    turned[...] = old * cos[:, None, :] + swapped * sin[:, None, :]
    for h in range(heads):
        q_out[tokens * h : tokens * (h + 1), :] = turned[:, h, :].astype(jnp.bfloat16)
    for copy in copies[1:]:
        copy.wait()


def prepare(queries, keys, values, fresh, positions):
    tokens, heads, width = queries.shape
    steps_index = jnp.arange(width // 2, dtype=jnp.float32)
    inverse = jnp.exp(steps_index * (-2.0 * math.log(ROPE_BASE) / width))
    angles = positions[:, None] * jnp.concatenate([inverse, inverse])[None, :]
    sign = jnp.where(jnp.arange(width) < width // 2, -1.0, 1.0).astype(jnp.float32)
    n = keys.shape[0]
    return pl.pallas_call(
        prepare_kernel,
        out_shape=(
            jax.ShapeDtypeStruct((tokens * heads, width), jnp.bfloat16),
            jax.ShapeDtypeStruct((2 * n + NOTE, width), jnp.bfloat16),
        ),
        in_specs=[HBM] * 3 + [VMEM] * 3,
        out_specs=(VMEM, VMEM),
        scratch_shapes=[
            pltpu.VMEM(queries.shape, jnp.bfloat16),
            pltpu.VMEM(queries.shape, jnp.float32),
            pltpu.SemaphoreType.DMA((9,)),
        ],
        compiler_params=pltpu.CompilerParams(vmem_limit_bytes=12 << 20),
        cost_estimate=pl.CostEstimate(flops=1 << 18, bytes_accessed=1 << 20, transcendentals=0),
        name="prepare",
    )(queries, keys, values, fresh, jnp.cos(angles), jnp.sin(angles) * sign)


def dot_nt(a, b):
    return lax.dot_general(a, b, (((1,), (1,)), ((), ())), preferred_element_type=jnp.float32)


NOTE = 48


def fill_bias(pack, n):
    fill = pack[2 * n + 32 : 2 * n + 48, :].astype(jnp.float32)[0:1, :]
    fill = jnp.concatenate([fill] * (n // HD), axis=1)
    row = lax.broadcasted_iota(jnp.int32, (1, n), 1).astype(jnp.float32)
    return jnp.where(row < fill, 0.0, NEG)


def absorb(state, scores, values):
    weigh = jnp.concatenate([values, jnp.ones_like(values)], axis=1)
    high = scores.max(axis=1, keepdims=True)
    if state is None:
        weights = jnp.exp2(scores - high).astype(jnp.bfloat16)
        return high, jnp.dot(weights, weigh, preferred_element_type=jnp.float32)
    top, acc = state
    high = jnp.maximum(top, high)
    weights = jnp.exp2(scores - high).astype(jnp.bfloat16)
    term = jnp.dot(weights, weigh, preferred_element_type=jnp.float32)
    return high, acc * jnp.exp2(top - high) + term


def sweep(states, tiles, packs):
    scale = LOG2E / math.sqrt(HD)
    for pack in packs:
        n = (pack.shape[0] - NOTE) // 2
        block = min(512, n)
        bias = fill_bias(pack, n)
        for b in range(0, n, block):
            for t, q in enumerate(tiles):
                scores = dot_nt(q, pack[b : b + block, :]) * scale + bias[:, b : b + block]
                states[t] = absorb(states[t], scores, pack[n + b : n + b + block, :])
    return states


def tile_groups(q_refs):
    whole = q_refs[0].shape[0]
    even = len(q_refs) // 2 * 2
    groups = [((i, 0, whole), (i + 1, 0, whole)) for i in range(0, even, 2)]
    if even < len(q_refs):
        groups.append(((even, 0, whole // 2), (even, whole // 2, whole // 2)))
    return groups


def first_kernel(chunks, *refs):
    q_refs, refs = refs[:chunks], refs[chunks:]
    packs, (acc_ref, top_ref) = refs[0:2], refs[2:]
    for group in tile_groups(q_refs):
        tiles = [q_refs[i][p : p + rows, :] for i, p, rows in group]
        states = sweep([None] * len(tiles), tiles, packs)
        for (i, p, rows), (top, acc) in zip(group, states):
            acc_ref[i, p : p + rows, :] = acc
            top_ref[i, p : p + rows, :] = jnp.broadcast_to(top, (rows, HD))


def flash_first(q_list, packs):
    chunks, rows = len(q_list), q_list[0].shape[0]
    keys = sum(pack.shape[0] - NOTE for pack in packs) // 2
    return pl.pallas_call(
        functools.partial(first_kernel, chunks),
        out_shape=(
            jax.ShapeDtypeStruct((chunks, rows, 2 * HD), jnp.float32),
            jax.ShapeDtypeStruct((chunks, rows, HD), jnp.float32),
        ),
        in_specs=[VMEM] * (chunks + 2),
        out_specs=(VMEM, VMEM),
        compiler_params=pltpu.CompilerParams(vmem_limit_bytes=14 << 20),
        cost_estimate=pl.CostEstimate(
            flops=chunks << 29, bytes_accessed=1 << 20, transcendentals=0
        ),
        name="flash_first",
    )(*q_list, *packs)


def pack_level(level, stat, first_row):
    line = lax.broadcasted_iota(jnp.int32, stat.shape, 0)
    for b in range(level.shape[0] // HD):
        flat = jnp.transpose(level[b * HD : (b + 1) * HD, :])[0:STAT, :]
        for t in range(3):
            piece = flat.astype(jnp.bfloat16).astype(jnp.float32)
            stat = jnp.where(line == 3 * (first_row // HD + b) + t, piece, stat)
            flat = flat - piece
    return stat


def place():
    me = lax.axis_index("ctx")
    return me >> 2, (me >> 1) & 1, me & 1


def second_kernel(offsets, shards, first, *refs):
    chunks = len(offsets)
    q_refs, refs = refs[:chunks], refs[chunks:]
    acc_ref, top_ref, packs = refs[0], refs[1], refs[2:6]
    out_refs, (new_k, new_v) = refs[6 : 6 + chunks], refs[6 + chunks :]
    n = (packs[0].shape[0] - NOTE) // 2
    new_k[...] = jnp.zeros_like(new_k)
    new_v[...] = jnp.zeros_like(new_v)
    for s, pack in enumerate(packs):
        new_k[16 * s : 16 * s + 16, :] = pack[2 * n : 2 * n + 16, :]
        new_v[16 * s : 16 * s + 16, :] = pack[2 * n + 16 : 2 * n + 32, :]
    scale = LOG2E / math.sqrt(HD)
    my_z, my_x, my_c = place()
    column = lax.broadcasted_iota(jnp.int32, (1, HD), 1)
    key_token = (
        64 * my_z
        + 32 * (my_x ^ (column >> 5))
        + 16 * (my_c ^ ((column >> 4) & 1))
        + (column & 15)
    )
    key_token = jnp.where(column < 64, key_token, 1 << 20)
    stats = [jnp.zeros((STAT, HD), jnp.float32) for _ in q_refs]
    for group in tile_groups(q_refs):
        tiles = [q_refs[i][p : p + rows, :] for i, p, rows in group]
        states = []
        for tile, (i, p, rows) in zip(tiles, group):
            home = lax.rem(my_z + offsets[i] + shards, shards)
            row_token = lax.broadcasted_iota(jnp.int32, (rows, HD), 0) & 15
            row_token = row_token + (64 * home + 32 * my_x + 16 * my_c)
            scores = dot_nt(tile, new_k[...]) * scale
            scores = jnp.where(key_token <= row_token, scores, NEG)
            states.append(absorb(None, scores, new_v[...]))
        states = sweep(states, tiles, packs[2:])
        for (i, p, rows), (top, acc) in zip(group, states):
            near_top = top_ref[first + i, p : p + rows, :]
            top = jnp.broadcast_to(top, near_top.shape)
            high = jnp.maximum(top, near_top)
            near, far = jnp.exp2(near_top - high), jnp.exp2(top - high)
            near_acc = acc_ref[first + i, p : p + rows, :]
            total = near * near_acc[:, HD:] + far * acc[:, HD:]
            mean = (near * near_acc[:, :HD] + far * acc[:, :HD]) / total
            out_refs[i][p : p + rows, :] = mean.astype(jnp.bfloat16)
            stats[i] = pack_level(high + jnp.log2(total), stats[i], p)
    for i, out in enumerate(out_refs):
        whole = q_refs[i].shape[0]
        out[whole : whole + STAT, :] = stats[i].astype(jnp.bfloat16)


def flash_second(offsets, shards, q_list, state, first, packs):
    chunks, rows = len(q_list), q_list[0].shape[0]
    keys = packs[0].shape[0]
    return pl.pallas_call(
        functools.partial(second_kernel, offsets, shards, first),
        out_shape=[jax.ShapeDtypeStruct((rows + STAT, HD), jnp.bfloat16)] * chunks,
        in_specs=[VMEM] * (chunks + 6),
        out_specs=[VMEM] * chunks,
        scratch_shapes=[pltpu.VMEM((HD, HD), jnp.bfloat16), pltpu.VMEM((HD, HD), jnp.bfloat16)],
        compiler_params=pltpu.CompilerParams(vmem_limit_bytes=14 << 20),
        cost_estimate=pl.CostEstimate(flops=1 << 20, bytes_accessed=1 << 16, transcendentals=0),
        name="flash_second",
    )(*q_list, *state, *packs)


def merge_kernel(sizes, final, *refs):
    in_refs, out_refs = refs[: sum(sizes)], refs[sum(sizes) :]
    for size, out_ref in zip(sizes, out_refs):
        parts, in_refs = in_refs[:size], in_refs[size:]
        rows = parts[0].shape[0] - STAT
        packed = jnp.zeros((STAT, HD), jnp.float32)
        for b in range(rows // HD):
            levels = []
            for part in parts:
                stat = part[rows : rows + STAT, :].astype(jnp.float32)[3 * b : 3 * b + 3]
                flat = stat[0:1] + stat[1:2] + stat[2:3]
                levels.append(jnp.transpose(jnp.broadcast_to(flat, (HD, HD))))
            top = functools.reduce(jnp.maximum, levels)
            total = jnp.zeros((HD, HD), jnp.float32)
            acc = jnp.zeros((HD, HD), jnp.float32)
            for part, level in zip(parts, levels):
                share = jnp.exp2(level - top)
                total = total + share
                acc = acc + share * part[b * HD : (b + 1) * HD, :].astype(jnp.float32)
            out_ref[b * HD : (b + 1) * HD, :] = (acc / total).astype(jnp.bfloat16)
            packed = pack_level(top + jnp.log2(total), packed, b * HD)
        if not final:
            out_ref[rows : rows + STAT, :] = packed.astype(jnp.bfloat16)


def merge(groups, final=False):
    parts = [part for group in groups for part in group]
    rows = parts[0].shape[0] - (STAT if final else 0)
    return pl.pallas_call(
        functools.partial(merge_kernel, [len(group) for group in groups], final),
        out_shape=[jax.ShapeDtypeStruct((rows, HD), jnp.bfloat16)] * len(groups),
        in_specs=[VMEM] * len(parts),
        out_specs=[VMEM] * len(groups),
        compiler_params=pltpu.CompilerParams(vmem_limit_bytes=12 << 20),
        cost_estimate=pl.CostEstimate(flops=1 << 20, bytes_accessed=1 << 16, transcendentals=0),
        name="merge",
    )(*parts)


def project_kernel(chunks, *refs):
    pair_refs, (w_own, w_core, out_ref, left_ref) = refs[:chunks], refs[chunks:]
    my_z, my_x, _ = place()
    heads = left_ref.shape[3] // HD
    for i in range(chunks):
        home = lax.rem(my_z + i, chunks)
        for k in range(2):
            for h in range(heads):
                first = (k * heads + h) * 16
                left_ref[home, my_x ^ k, :, h * HD : (h + 1) * HD] = pair_refs[i][
                    first : first + 16, :
                ]
    left = left_ref[...].reshape(chunks * 32, heads * HD)
    width = w_own.shape[1]
    for k, w in enumerate((w_own, w_core)):
        terms = jnp.dot(left, w[...], preferred_element_type=jnp.float32)
        out_ref[:, :, k * width : (k + 1) * width] = terms.astype(jnp.bfloat16).reshape(
            chunks, 32, width
        )


def project(pairs, w_own, w_core):
    chunks = len(pairs)
    depth, width = w_own.shape
    return pl.pallas_call(
        functools.partial(project_kernel, chunks),
        out_shape=jax.ShapeDtypeStruct((chunks, 32, 2 * width), jnp.bfloat16),
        in_specs=[VMEM] * (chunks + 2),
        out_specs=VMEM,
        scratch_shapes=[pltpu.VMEM((chunks, 2, 16, depth), jnp.bfloat16)],
        compiler_params=pltpu.CompilerParams(vmem_limit_bytes=14 << 20),
        cost_estimate=pl.CostEstimate(
            flops=2 * chunks * 32 * depth * 2 * width, bytes_accessed=6 << 20, transcendentals=0
        ),
        name="project",
    )(*pairs, w_own, w_core)


def on_device(
    queries, cache_keys, cache_values, new_keys, new_values, fill_rows, turn_start, out_weight
):
    tok_dev, group_size, head_width = queries.shape
    ctx_count = lax.axis_size("ctx")
    shards = ctx_count // 4
    me = lax.axis_index("ctx")
    my_z, my_x, my_c = me // 4, (me // 2) % 2, me % 2
    cache_rows = cache_keys.shape[0]

    def permutation(dz, dx, dc):
        place = lambda z, x, c: ((z % shards) * 2 + x) * 2 + c
        return [
            (place(z, x, c), place(z + dz, x ^ dx, c ^ dc))
            for z in range(shards)
            for x in range(2)
            for c in range(2)
        ]

    def send(value, dz=0, dx=0, dc=0):
        return lax.ppermute(value, "ctx", permutation(dz, dx, dc))

    def after(value, *others):
        return lax.optimization_barrier((value,) + others)[0]

    positions = (turn_start[0] + me * tok_dev + jnp.arange(tok_dev, dtype=jnp.int32)).astype(
        jnp.float32
    )
    q = {}
    fresh = jnp.concatenate(
        [
            new_keys.reshape(tok_dev, head_width),
            new_values.reshape(tok_dev, head_width),
            jnp.full((16, head_width), fill_rows[0].astype(jnp.bfloat16)),
        ],
        axis=0,
    )
    q[0], pack = prepare(
        queries,
        cache_keys.reshape(cache_rows, head_width),
        cache_values.reshape(cache_rows, head_width),
        fresh,
        positions,
    )
    pack_x, pack_c = send(pack, dx=1), send(pack, dc=1)
    for d in (1, -1, 2, -2):
        q[d] = send(q[0], dz=-d)
    here, close, wide, outer = (0,), (1, -1), (2, -2), (3, -3, 4)
    state = {here: flash_first([q[0]], (pack, pack_c))}
    arrived = (q[1], q[-1], state[here][1])
    pack_x = after(pack_x, q[2], q[-2], *arrived)
    pack_xc = send(pack_x, dc=1)
    up, down = after(q[2], q[-2], *arrived), after(q[-2], q[2], *arrived)
    q[3], q[-3], q[4] = send(up, dz=-1), send(down, dz=1), send(up, dz=-2)
    both = flash_first([q[d] for d in close + wide], (pack, pack_c))
    state[close], state[wide] = both, both
    q[-3] = after(q[-3], both[1])
    state[outer] = flash_first([q[d] for d in outer], (pack, pack_c))
    packs = (pack, pack_c, pack_x, pack_xc)

    part = {}

    def finish(offsets, first=0):
        chunks = [q[d] for d in offsets]
        done = flash_second(offsets, shards, chunks, state[offsets], first, packs)
        part.update(zip(offsets, done))

    finish(outer)
    from_3, from_4, from_m3 = send(part[3], dz=1), send(part[4], dz=2), send(part[-3], dz=-1)
    finish(wide, 2)
    q[1] = after(q[1], part[2])
    finish(close)
    got = [send(part[1], dz=1), send(part[-1], dz=-1)]
    part[2] = after(part[2], part[1])
    up, down = merge([[part[2], from_3, from_4], [part[-2], from_m3]])
    got += [send(up, dz=2), send(down, dz=-2)]
    q[0] = after(q[0], up)
    finish(here)
    attention = merge([[part[0]] + got], final=True)[0]

    pair = {0: jnp.concatenate([attention, send(attention, dx=1)], axis=0)}
    for d in (1, -1, 2, -2):
        pair[d] = send(pair[0], dz=-d)
    pair[3], pair[-3], pair[4] = send(pair[2], dz=-1), send(pair[-2], dz=1), send(pair[2], dz=-2)
    w_core = send(out_weight, dc=1)
    terms = project([pair[d if d <= 4 else d - 8] for d in range(8)], out_weight, w_core)
    summed = (
        lax.all_to_all(terms, "kvh", 0, 0, tiled=True)
        .astype(jnp.float32)
        .sum(axis=0)
        .astype(jnp.bfloat16)
    )
    width = out_weight.shape[1]
    mine = summed[:, :width].reshape(2, 1, tok_dev, width)
    other = send(summed[:, width:], dc=1).reshape(2, 1, tok_dev, width)
    ordered = jnp.where(
        my_c == 0,
        jnp.concatenate([mine, other], axis=1),
        jnp.concatenate([other, mine], axis=1),
    )
    return ordered.reshape(4 * tok_dev, width)


def solution(mesh):
    in_specs = (
        P("ctx", "kvh", None),
        P("ctx", "kvh", None),
        P("ctx", "kvh", None),
        P("ctx", "kvh", None),
        P("ctx", "kvh", None),
        P("ctx"),
        P(),
        P("kvh", "ctx"),
    )
    out_specs = P("kvh", "ctx")
    return jax.shard_map(
        on_device, mesh=mesh, in_specs=in_specs, out_specs=out_specs, check_vma=False
    )
```

profile of v0, /device:TPU:1, one launch (start us, length us, event | category | flops | bytes accessed | tf_op | source)
XLA Modules:
  0.0 102.8 jit_solution(586307568011716851)
XLA Ops:
  0.0 3.2 %collective-permute-start.25 = (bf16[2048,512]{1,0:T(8,128)(2,1)}, bf16[2048,512]{1,0:T(8,128)(2,1)S(1)}, u32[]{:S(2)}, u32[]{:S(2)}) collective-permute-start(bf16[2048,512]{1,0:T(8,128)(2,1)} %refs_8_.1), channel_id=1, source_target_pairs={{0,8},{8,0},{16,24},{24,16},{32,40},{40,32},{48,56},{56,48},{64,72... | collective-permute-start | bytes 6291464 | tf_op jit(solution)/shard_map/ppermute | solution.py:327
  4.6 0.1 pad.10.clone
  4.6 0.8 maximum_maximum_fusion.fresh
  5.4 0.1 compare_select_fusion
  5.5 0.1 fusion
  5.6 0.0 copy-start.1
  5.6 0.9 copy-done.1
  6.6 0.9 copy-done.2
  7.5 0.8 copy-done.3
  8.4 1.1 %prepare.1 = (bf16[256,128]{1,0:T(8,128)(2,1)S(1)}, bf16[2096,128]{1,0:T(8,128)(2,1)S(1)}) custom-call(bf16[16,16,128]{2,1,0:T(8,128)(2,1)S(1)} %copy-done.3, bf16[1024,128]{1,0:T(8,128)(2,1)S(1)} %bitcast.10, bf16[1024,128]{1,0:T(8,128)(2,1)S(1)} %bitcast.11, bf16[48,128]{1,0:T(8,128)(2,1)S(1)} %maximum_maximum_fusion.fresh, ...), custom_call_target="tpu_custom_call" | custom-call | flops 262144 | bytes 1048576 | tf_op jit(solution)/shard_map/prepare/pallas_call | solution.py:53
  9.5 0.1 collective-permute-start.4
  9.6 1.1 %collective-permute-start.5 = (bf16[2096,128]{1,0:T(8,128)(2,1)S(1)}, bf16[2096,128]{1,0:T(8,128)(2,1)S(1)}, u32[]{:S(2)}, u32[]{:S(2)}) collective-permute-start(bf16[2096,128]{1,0:T(8,128)(2,1)S(1)} %get-tuple-element.30.refs_4_.refs_1_.refs_3_.refs_5_), channel_id=1, source_target_pairs={{0,16},{8,24},{16,0},{24,8},{32,48},{40,56},{48,32},{56,40},{64,80... | collective-permute-start | bytes 1609736 | tf_op jit(solution)/shard_map/ppermute | solution.py:327
  10.7 6.0 %collective-permute-start = (bf16[256,128]{1,0:T(8,128)(2,1)S(1)}, bf16[256,128]{1,0:T(8,128)(2,1)S(1)}, u32[]{:S(2)}, u32[]{:S(2)}) collective-permute-start(bf16[256,128]{1,0:T(8,128)(2,1)S(1)} %get-tuple-element.49.refs_0_), channel_id=1, source_target_pairs={{0,192},{8,200},{16,208},{24,216},{32,224},{40,232},{48,240},{56,2... | collective-permute-start | bytes 196616 | tf_op jit(solution)/shard_map/ppermute | solution.py:327
  16.7 0.0 collective-permute-start.1
  16.7 1.3 %collective-permute-done.refs_2_.refs_0_ = bf16[256,128]{1,0:T(8,128)(2,1)S(1)} collective-permute-done((bf16[256,128]{1,0:T(8,128)(2,1)S(1)}, bf16[256,128]{1,0:T(8,128)(2,1)S(1)}, u32[]{:S(2)}, u32[]{:S(2)}) %collective-permute-start) | collective-permute-done | bytes 65568 | tf_op jit(solution)/shard_map/ppermute | solution.py:327
  18.1 3.7 %collective-permute-start.2 = (bf16[256,128]{1,0:T(8,128)(2,1)S(1)}, bf16[256,128]{1,0:T(8,128)(2,1)S(1)}, u32[]{:S(2)}, u32[]{:S(2)}) collective-permute-start(bf16[256,128]{1,0:T(8,128)(2,1)S(1)} %get-tuple-element.49.refs_0_), channel_id=1, source_target_pairs={{0,224},{8,232},{16,240},{24,248},{32,0},{40,8},{48,16},{56,24},{6... | collective-permute-start | bytes 196616 | tf_op jit(solution)/shard_map/ppermute | solution.py:327
  21.8 0.0 collective-permute-done.4.refs_5_.refs_2_.refs_4_.refs_6_
  21.8 1.0 flash_first.4
  22.8 0.2 collective-permute-done.1.refs_3_.refs_1_
  22.9 0.2 collective-permute-done.2.refs_0_
  23.1 3.0 %collective-permute-done.3.refs_1_ = bf16[256,128]{1,0:T(8,128)(2,1)S(1)} collective-permute-done((bf16[256,128]{1,0:T(8,128)(2,1)S(1)}, bf16[256,128]{1,0:T(8,128)(2,1)S(1)}, u32[]{:S(2)}, u32[]{:S(2)}) %collective-permute-start.3) | collective-permute-done | bytes 65568 | tf_op jit(solution)/shard_map/ppermute | solution.py:327
  26.1 3.0 %collective-permute-start.6 = (bf16[2096,128]{1,0:T(8,128)(2,1)S(1)}, bf16[2096,128]{1,0:T(8,128)(2,1)S(1)}, u32[]{:S(2)}, u32[]{:S(2)}) collective-permute-start(bf16[2096,128]{1,0:T(8,128)(2,1)S(1)} %collective-permute-done.5.refs_6_.refs_7_.refs_5_), channel_id=1, source_target_pairs={{0,8},{8,0},{16,24},{24,16},{32,40},{40,32},{48,56},{56,48},{64,72... | collective-permute-start | bytes 1609736 | tf_op jit(solution)/shard_map/ppermute | solution.py:327
  29.1 0.5 collective-permute-start.7
  29.6 1.2 %collective-permute-start.9 = (bf16[256,128]{1,0:T(8,128)(2,1)S(1)}, bf16[256,128]{1,0:T(8,128)(2,1)S(1)}, u32[]{:S(2)}, u32[]{:S(2)}) collective-permute-start(bf16[256,128]{1,0:T(8,128)(2,1)S(1)} %collective-permute-done.refs_2_.refs_0_), channel_id=1, source_target_pairs={{0,192},{8,200},{16,208},{24,216},{32,224},{40,232},{48,240},{56,2... | collective-permute-start | bytes 196616 | tf_op jit(solution)/shard_map/ppermute | solution.py:327
  30.8 0.7 collective-permute-start.8
  31.6 3.0 %flash_first.3 = (f32[4,256,256]{2,1,0:T(8,128)S(1)}, f32[4,256,128]{2,1,0:T(8,128)S(1)}) custom-call(bf16[256,128]{1,0:T(8,128)(2,1)S(1)} %collective-permute-done.2.refs_0_, bf16[256,128]{1,0:T(8,128)(2,1)S(1)} %collective-permute-done.3.refs_1_, bf16[256,128]{1,0:T(8,128)(2,1)S(1)} %collective-permute-done.refs_2_.refs_0_, ...), custom_call_target="tpu_custom_call" | custom-call | flops 2147483648 | bytes 1048576 | tf_op jit(solution)/shard_map/flash_first/pallas_call | solution.py:135
  34.6 0.6 collective-permute-done.8.refs_1_
  35.1 2.5 %flash_first.5 = (f32[3,256,256]{2,1,0:T(8,128)S(1)}, f32[3,256,128]{2,1,0:T(8,128)S(1)}) custom-call(bf16[256,128]{1,0:T(8,128)(2,1)S(1)} %collective-permute-done.7.refs_0_, bf16[256,128]{1,0:T(8,128)(2,1)S(1)} %collective-permute-done.8.refs_1_, bf16[256,128]{1,0:T(8,128)(2,1)S(1)} %collective-permute-done.9.refs_2_, ...), custom_call_target="tpu_custom_call" | custom-call | flops 1610612736 | bytes 1048576 | tf_op jit(solution)/shard_map/flash_first/pallas_call | solution.py:135
  37.6 3.0 %flash_second.6 = (bf16[272,128]{1,0:T(8,128)(2,1)S(1)}, bf16[272,128]{1,0:T(8,128)(2,1)S(1)}, bf16[272,128]{1,0:T(8,128)(2,1)S(1)}) custom-call(bf16[256,128]{1,0:T(8,128)(2,1)S(1)} %collective-permute-done.7.refs_0_, bf16[256,128]{1,0:T(8,128)(2,1)S(1)} %collective-permute-done.8.refs_1_, bf16[256,128]{1,0:T(8,128)(2,1)S(1)} %collective-permute-done.9.refs_2_, ...), custom_call_target="tpu_custom_call" | custom-call | flops 1048576 | bytes 65536 | tf_op jit(solution)/shard_map/flash_second/pallas_call | solution.py:218
  40.6 1.5 %collective-permute-start.10 = (bf16[272,128]{1,0:T(8,128)(2,1)S(1)}, bf16[272,128]{1,0:T(8,128)(2,1)S(1)}, u32[]{:S(2)}, u32[]{:S(2)}) collective-permute-start(bf16[272,128]{1,0:T(8,128)(2,1)S(1)} %get-tuple-element.44), channel_id=1, source_target_pairs={{0,32},{8,40},{16,48},{24,56},{32,64},{40,72},{48,80},{56,88},{64,... | collective-permute-start | bytes 208904 | tf_op jit(solution)/shard_map/ppermute | solution.py:327
  42.1 0.3 collective-permute-start.11
  42.4 2.2 %collective-permute-start.12 = (bf16[272,128]{1,0:T(8,128)(2,1)S(1)}, bf16[272,128]{1,0:T(8,128)(2,1)S(1)}, u32[]{:S(2)}, u32[]{:S(2)}) collective-permute-start(bf16[272,128]{1,0:T(8,128)(2,1)S(1)} %get-tuple-element.47), channel_id=1, source_target_pairs={{0,224},{8,232},{16,240},{24,248},{32,0},{40,8},{48,16},{56,24},{6... | collective-permute-start | bytes 208904 | tf_op jit(solution)/shard_map/ppermute | solution.py:327
  44.6 2.0 %flash_second.4 = (bf16[272,128]{1,0:T(8,128)(2,1)S(1)}, bf16[272,128]{1,0:T(8,128)(2,1)S(1)}) custom-call(bf16[256,128]{1,0:T(8,128)(2,1)S(1)} %collective-permute-done.refs_2_.refs_0_, bf16[256,128]{1,0:T(8,128)(2,1)S(1)} %collective-permute-done.1.refs_3_.refs_1_, f32[4,256,256]{2,1,0:T(8,128)S(1)} %get-tuple-element.31.refs_2_, ...), custom_call_target="tpu_custom_call" | custom-call | flops 1048576 | bytes 65536 | tf_op jit(solution)/shard_map/flash_second/pallas_call | solution.py:218
  46.6 2.0 %flash_second.5 = (bf16[272,128]{1,0:T(8,128)(2,1)S(1)}, bf16[272,128]{1,0:T(8,128)(2,1)S(1)}) custom-call(bf16[256,128]{1,0:T(8,128)(2,1)S(1)} %collective-permute-done.2.refs_0_, bf16[256,128]{1,0:T(8,128)(2,1)S(1)} %collective-permute-done.3.refs_1_, f32[4,256,256]{2,1,0:T(8,128)S(1)} %get-tuple-element.31.refs_2_, ...), custom_call_target="tpu_custom_call" | custom-call | flops 1048576 | bytes 65536 | tf_op jit(solution)/shard_map/flash_second/pallas_call | solution.py:218
  48.6 0.0 copy-start
  48.7 0.1 collective-permute-start.13
  48.8 2.7 %collective-permute-start.14 = (bf16[272,128]{1,0:T(8,128)(2,1)S(1)}, bf16[272,128]{1,0:T(8,128)(2,1)S(1)}, u32[]{:S(2)}, u32[]{:S(2)}) collective-permute-start(bf16[272,128]{1,0:T(8,128)(2,1)S(1)} %get-tuple-element.51), channel_id=1, source_target_pairs={{0,224},{8,232},{16,240},{24,248},{32,0},{40,8},{48,16},{56,24},{6... | collective-permute-start | bytes 208904 | tf_op jit(solution)/shard_map/ppermute | solution.py:327
  51.4 0.4 merge.2
  51.9 0.1 collective-permute-start.15
  51.9 3.6 %collective-permute-start.16 = (bf16[272,128]{1,0:T(8,128)(2,1)S(1)}, bf16[272,128]{1,0:T(8,128)(2,1)S(1)}, u32[]{:S(2)}, u32[]{:S(2)}) collective-permute-start(bf16[272,128]{1,0:T(8,128)(2,1)S(1)} %get-tuple-element.52), channel_id=1, source_target_pairs={{0,192},{8,200},{16,208},{24,216},{32,224},{40,232},{48,240},{56,2... | collective-permute-start | bytes 208904 | tf_op jit(solution)/shard_map/ppermute | solution.py:327
  55.5 1.5 %flash_second.7.refs_0_ = bf16[272,128]{1,0:T(8,128)(2,1)S(1)} custom-call(bf16[256,128]{1,0:T(8,128)(2,1)S(1)} %get-tuple-element.49.refs_0_, f32[1,256,256]{2,1,0:T(8,128)S(1)} %get-tuple-element.50.refs_1_, f32[1,256,128]{2,1,0:T(8,128)S(1)} %get-tuple-element.33.refs_2_, bf16[2096,128]{1,0:T(8,128)(2,1)S(1)} %get-tuple-element.30.refs_4_.refs_1_.refs_3_.refs_5_, ...), custom_call_target="tpu_custom_call" | custom-call | flops 1048576 | bytes 65536 | tf_op jit(solution)/shard_map/flash_second/pallas_call | solution.py:218
  57.0 0.4 collective-permute-done.15.refs_3_
  57.5 0.3 merge.3
  57.8 2.9 %collective-permute-start.17 = (bf16[256,128]{1,0:T(8,128)(2,1)S(1)}, bf16[256,128]{1,0:T(8,128)(2,1)S(1)}, u32[]{:S(2)}, u32[]{:S(2)}) collective-permute-start(bf16[256,128]{1,0:T(8,128)(2,1)S(1)} %merge.3), channel_id=1, source_target_pairs={{0,16},{8,24},{16,0},{24,8},{32,48},{40,56},{48,32},{56,40},{64,80... | collective-permute-start | bytes 196616 | tf_op jit(solution)/shard_map/ppermute | solution.py:327
  60.7 1.8 %collective-permute-done.17 = bf16[256,128]{1,0:T(8,128)(2,1)S(1)} collective-permute-done((bf16[256,128]{1,0:T(8,128)(2,1)S(1)}, bf16[256,128]{1,0:T(8,128)(2,1)S(1)}, u32[]{:S(2)}, u32[]{:S(2)}) %collective-permute-start.17) | collective-permute-done | bytes 65568 | tf_op jit(solution)/shard_map/ppermute | solution.py:327
  62.5 3.4 %collective-permute-start.19 = (bf16[512,128]{1,0:T(8,128)(2,1)S(1)}, bf16[512,128]{1,0:T(8,128)(2,1)S(1)}, u32[]{:S(2)}, u32[]{:S(2)}) collective-permute-start(bf16[512,128]{1,0:T(8,128)(2,1)S(1)} %pad_maximum_fusion.refs_0_), channel_id=1, source_target_pairs={{0,192},{8,200},{16,208},{24,216},{32,224},{40,232},{48,240},{56,2... | collective-permute-start | bytes 393224 | tf_op jit(solution)/shard_map/ppermute | solution.py:327
  65.9 0.2 collective-permute-start.22
  66.0 1.4 %collective-permute-start.24 = (bf16[512,128]{1,0:T(8,128)(2,1)S(1)}, bf16[512,128]{1,0:T(8,128)(2,1)S(1)}, u32[]{:S(2)}, u32[]{:S(2)}) collective-permute-start(bf16[512,128]{1,0:T(8,128)(2,1)S(1)} %pad_maximum_fusion.refs_0_), channel_id=1, source_target_pairs={{0,32},{8,40},{16,48},{24,56},{32,64},{40,72},{48,80},{56,88},{64,... | collective-permute-start | bytes 393224 | tf_op jit(solution)/shard_map/ppermute | solution.py:327
  67.4 2.1 %collective-permute-done.19.refs_2_ = bf16[512,128]{1,0:T(8,128)(2,1)S(1)} collective-permute-done((bf16[512,128]{1,0:T(8,128)(2,1)S(1)}, bf16[512,128]{1,0:T(8,128)(2,1)S(1)}, u32[]{:S(2)}, u32[]{:S(2)}) %collective-permute-start.19) | collective-permute-done | bytes 131104 | tf_op jit(solution)/shard_map/ppermute | solution.py:327
  69.5 0.3 collective-permute-start.20
  69.7 1.4 %collective-permute-done.18.refs_1_ = bf16[512,128]{1,0:T(8,128)(2,1)S(1)} collective-permute-done((bf16[512,128]{1,0:T(8,128)(2,1)S(1)}, bf16[512,128]{1,0:T(8,128)(2,1)S(1)}, u32[]{:S(2)}, u32[]{:S(2)}) %collective-permute-start.18) | collective-permute-done | bytes 131104 | tf_op jit(solution)/shard_map/ppermute | solution.py:327
  71.1 0.9 collective-permute-start.21
  72.0 0.9 collective-permute-done.22.refs_6_
  72.9 1.8 %collective-permute-start.23 = (bf16[512,128]{1,0:T(8,128)(2,1)S(1)}, bf16[512,128]{1,0:T(8,128)(2,1)S(1)}, u32[]{:S(2)}, u32[]{:S(2)}) collective-permute-start(bf16[512,128]{1,0:T(8,128)(2,1)S(1)} %collective-permute-done.22.refs_6_), channel_id=1, source_target_pairs={{0,32},{8,40},{16,48},{24,56},{32,64},{40,72},{48,80},{56,88},{64,... | collective-permute-start | bytes 393224 | tf_op jit(solution)/shard_map/ppermute | solution.py:327
  74.7 0.1 collective-permute-done.24.refs_7_
  74.9 1.3 %collective-permute-done.20.refs_3_ = bf16[512,128]{1,0:T(8,128)(2,1)S(1)} collective-permute-done((bf16[512,128]{1,0:T(8,128)(2,1)S(1)}, bf16[512,128]{1,0:T(8,128)(2,1)S(1)}, u32[]{:S(2)}, u32[]{:S(2)}) %collective-permute-start.20) | collective-permute-done | bytes 131104 | tf_op jit(solution)/shard_map/ppermute | solution.py:327
  76.1 4.1 %collective-permute-done.21.refs_4_ = bf16[512,128]{1,0:T(8,128)(2,1)S(1)} collective-permute-done((bf16[512,128]{1,0:T(8,128)(2,1)S(1)}, bf16[512,128]{1,0:T(8,128)(2,1)S(1)}, u32[]{:S(2)}, u32[]{:S(2)}) %collective-permute-start.21) | collective-permute-done | bytes 131104 | tf_op jit(solution)/shard_map/ppermute | solution.py:327
  80.2 0.4 collective-permute-done.23.refs_5_
  80.5 1.4 %project.1 = bf16[8,32,1024]{2,1,0:T(8,128)(2,1)S(1)} custom-call(bf16[512,128]{1,0:T(8,128)(2,1)S(1)} %pad_maximum_fusion.refs_0_, bf16[512,128]{1,0:T(8,128)(2,1)S(1)} %collective-permute-done.18.refs_1_, bf16[512,128]{1,0:T(8,128)(2,1)S(1)} %collective-permute-done.19.refs_2_, bf16[512,128]{1,0:T(8,128)(2,1)S(1)} %collective-permute-done.20.refs_3_, ...), custom_call_target="tpu_custom_call" | custom-call | flops 1073741824 | bytes 6291456 | tf_op jit(solution)/shard_map/project/pallas_call | solution.py:293
  82.0 11.5 %all_to_all.5 = bf16[8,32,1024]{2,1,0:T(8,128)(2,1)S(1)} all-to-all(bf16[8,32,1024]{2,1,0:T(8,128)(2,1)S(1)} %project.1), channel_id=1, replica_groups=mesh['ctx'=32,'kvh'=8] {'kvh'}, dimensions={0} | all-to-all | bytes 1048576 | tf_op jit(solution)/shard_map/all_to_all | solution.py:394
  93.5 0.1 reduce_sum.12
  93.6 7.7 %collective-permute-start.26 = (bf16[32,512]{1,0:T(8,128)(2,1)S(1)}, bf16[32,512]{1,0:T(8,128)(2,1)S(1)}, u32[]{:S(2)}, u32[]{:S(2)}) collective-permute-start(bf16[32,512]{1,0:T(8,128)(2,1)S(1)} %get-tuple-element.54), channel_id=1, source_target_pairs={{0,8},{8,0},{16,24},{24,16},{32,40},{40,32},{48,56},{56,48},{64,72... | collective-permute-start | bytes 98312 | tf_op jit(solution)/shard_map/ppermute | solution.py:327
  101.3 0.9 collective-permute-done.26
  102.2 0.6 maximum_select_fusion
  (21 shorter events, 0.1 us)
Async XLA Ops:
  0.0 80.5 %collective-permute-start.25 = (bf16[2048,512]{1,0:T(8,128)(2,1)}, bf16[2048,512]{1,0:T(8,128)(2,1)S(1)}, u32[]{:S(2)}, u32[]{:S(2)}) collective-permute-start(bf16[2048,512]{1,0:T(8,128)(2,1)} %refs_8_.1), channel_id=1, source_target_pairs={{0,8},{8,0},{16,24},{24,16},{32,40},{40,32},{48,56},{56,48},{64,72... | collective-permute-start | bytes 6291464 | tf_op jit(solution)/shard_map/ppermute | solution.py:327
  5.6 1.0 copy-start.1
  6.6 0.9 copy-start.2
  7.5 0.8 copy-start.3
  9.5 12.3 %collective-permute-start.4 = (bf16[2096,128]{1,0:T(8,128)(2,1)S(1)}, bf16[2096,128]{1,0:T(8,128)(2,1)S(1)}, u32[]{:S(2)}, u32[]{:S(2)}) collective-permute-start(bf16[2096,128]{1,0:T(8,128)(2,1)S(1)} %get-tuple-element.30.refs_4_.refs_1_.refs_3_.refs_5_), channel_id=1, source_target_pairs={{0,8},{8,0},{16,24},{24,16},{32,40},{40,32},{48,56},{56,48},{64,72... | collective-permute-start | bytes 1609736 | tf_op jit(solution)/shard_map/ppermute | solution.py:327
  9.6 16.5 %collective-permute-start.5 = (bf16[2096,128]{1,0:T(8,128)(2,1)S(1)}, bf16[2096,128]{1,0:T(8,128)(2,1)S(1)}, u32[]{:S(2)}, u32[]{:S(2)}) collective-permute-start(bf16[2096,128]{1,0:T(8,128)(2,1)S(1)} %get-tuple-element.30.refs_4_.refs_1_.refs_3_.refs_5_), channel_id=1, source_target_pairs={{0,16},{8,24},{16,0},{24,8},{32,48},{40,56},{48,32},{56,40},{64,80... | collective-permute-start | bytes 1609736 | tf_op jit(solution)/shard_map/ppermute | solution.py:327
  10.7 7.4 %collective-permute-start = (bf16[256,128]{1,0:T(8,128)(2,1)S(1)}, bf16[256,128]{1,0:T(8,128)(2,1)S(1)}, u32[]{:S(2)}, u32[]{:S(2)}) collective-permute-start(bf16[256,128]{1,0:T(8,128)(2,1)S(1)} %get-tuple-element.49.refs_0_), channel_id=1, source_target_pairs={{0,192},{8,200},{16,208},{24,216},{32,224},{40,232},{48,240},{56,2... | collective-permute-start | bytes 196616 | tf_op jit(solution)/shard_map/ppermute | solution.py:327
  16.7 6.2 %collective-permute-start.1 = (bf16[256,128]{1,0:T(8,128)(2,1)S(1)}, bf16[256,128]{1,0:T(8,128)(2,1)S(1)}, u32[]{:S(2)}, u32[]{:S(2)}) collective-permute-start(bf16[256,128]{1,0:T(8,128)(2,1)S(1)} %get-tuple-element.49.refs_0_), channel_id=1, source_target_pairs={{0,64},{8,72},{16,80},{24,88},{32,96},{40,104},{48,112},{56,120},{... | collective-permute-start | bytes 196616 | tf_op jit(solution)/shard_map/ppermute | solution.py:327
  18.1 5.1 %collective-permute-start.2 = (bf16[256,128]{1,0:T(8,128)(2,1)S(1)}, bf16[256,128]{1,0:T(8,128)(2,1)S(1)}, u32[]{:S(2)}, u32[]{:S(2)}) collective-permute-start(bf16[256,128]{1,0:T(8,128)(2,1)S(1)} %get-tuple-element.49.refs_0_), channel_id=1, source_target_pairs={{0,224},{8,232},{16,240},{24,248},{32,0},{40,8},{48,16},{56,24},{6... | collective-permute-start | bytes 196616 | tf_op jit(solution)/shard_map/ppermute | solution.py:327
  21.8 4.3 %collective-permute-start.3 = (bf16[256,128]{1,0:T(8,128)(2,1)S(1)}, bf16[256,128]{1,0:T(8,128)(2,1)S(1)}, u32[]{:S(2)}, u32[]{:S(2)}) collective-permute-start(bf16[256,128]{1,0:T(8,128)(2,1)S(1)} %get-tuple-element.49.refs_0_), channel_id=1, source_target_pairs={{0,32},{8,40},{16,48},{24,56},{32,64},{40,72},{48,80},{56,88},{64,... | collective-permute-start | bytes 196616 | tf_op jit(solution)/shard_map/ppermute | solution.py:327
  26.1 11.5 %collective-permute-start.6 = (bf16[2096,128]{1,0:T(8,128)(2,1)S(1)}, bf16[2096,128]{1,0:T(8,128)(2,1)S(1)}, u32[]{:S(2)}, u32[]{:S(2)}) collective-permute-start(bf16[2096,128]{1,0:T(8,128)(2,1)S(1)} %collective-permute-done.5.refs_6_.refs_7_.refs_5_), channel_id=1, source_target_pairs={{0,8},{8,0},{16,24},{24,16},{32,40},{40,32},{48,56},{56,48},{64,72... | collective-permute-start | bytes 1609736 | tf_op jit(solution)/shard_map/ppermute | solution.py:327
  29.1 6.0 %collective-permute-start.7 = (bf16[256,128]{1,0:T(8,128)(2,1)S(1)}, bf16[256,128]{1,0:T(8,128)(2,1)S(1)}, u32[]{:S(2)}, u32[]{:S(2)}) collective-permute-start(bf16[256,128]{1,0:T(8,128)(2,1)S(1)} %collective-permute-done.refs_2_.refs_0_), channel_id=1, source_target_pairs={{0,224},{8,232},{16,240},{24,248},{32,0},{40,8},{48,16},{56,24},{6... | collective-permute-start | bytes 196616 | tf_op jit(solution)/shard_map/ppermute | solution.py:327
  29.6 5.5 %collective-permute-start.9 = (bf16[256,128]{1,0:T(8,128)(2,1)S(1)}, bf16[256,128]{1,0:T(8,128)(2,1)S(1)}, u32[]{:S(2)}, u32[]{:S(2)}) collective-permute-start(bf16[256,128]{1,0:T(8,128)(2,1)S(1)} %collective-permute-done.refs_2_.refs_0_), channel_id=1, source_target_pairs={{0,192},{8,200},{16,208},{24,216},{32,224},{40,232},{48,240},{56,2... | collective-permute-start | bytes 196616 | tf_op jit(solution)/shard_map/ppermute | solution.py:327
  30.8 4.3 %collective-permute-start.8 = (bf16[256,128]{1,0:T(8,128)(2,1)S(1)}, bf16[256,128]{1,0:T(8,128)(2,1)S(1)}, u32[]{:S(2)}, u32[]{:S(2)}) collective-permute-start(bf16[256,128]{1,0:T(8,128)(2,1)S(1)} %collective-permute-done.1.refs_3_.refs_1_), channel_id=1, source_target_pairs={{0,32},{8,40},{16,48},{24,56},{32,64},{40,72},{48,80},{56,88},{64,... | collective-permute-start | bytes 196616 | tf_op jit(solution)/shard_map/ppermute | solution.py:327
  40.6 8.1 %collective-permute-start.10 = (bf16[272,128]{1,0:T(8,128)(2,1)S(1)}, bf16[272,128]{1,0:T(8,128)(2,1)S(1)}, u32[]{:S(2)}, u32[]{:S(2)}) collective-permute-start(bf16[272,128]{1,0:T(8,128)(2,1)S(1)} %get-tuple-element.44), channel_id=1, source_target_pairs={{0,32},{8,40},{16,48},{24,56},{32,64},{40,72},{48,80},{56,88},{64,... | collective-permute-start | bytes 208904 | tf_op jit(solution)/shard_map/ppermute | solution.py:327
  42.1 9.3 %collective-permute-start.11 = (bf16[272,128]{1,0:T(8,128)(2,1)S(1)}, bf16[272,128]{1,0:T(8,128)(2,1)S(1)}, u32[]{:S(2)}, u32[]{:S(2)}) collective-permute-start(bf16[272,128]{1,0:T(8,128)(2,1)S(1)} %get-tuple-element.45), channel_id=1, source_target_pairs={{0,64},{8,72},{16,80},{24,88},{32,96},{40,104},{48,112},{56,120},{... | collective-permute-start | bytes 208904 | tf_op jit(solution)/shard_map/ppermute | solution.py:327
  42.4 9.1 %collective-permute-start.12 = (bf16[272,128]{1,0:T(8,128)(2,1)S(1)}, bf16[272,128]{1,0:T(8,128)(2,1)S(1)}, u32[]{:S(2)}, u32[]{:S(2)}) collective-permute-start(bf16[272,128]{1,0:T(8,128)(2,1)S(1)} %get-tuple-element.47), channel_id=1, source_target_pairs={{0,224},{8,232},{16,240},{24,248},{32,0},{40,8},{48,16},{56,24},{6... | collective-permute-start | bytes 208904 | tf_op jit(solution)/shard_map/ppermute | solution.py:327
  48.6 31.9 %copy-start = (bf16[2048,512]{1,0:T(8,128)(2,1)S(1)}, bf16[2048,512]{1,0:T(8,128)(2,1)}, u32[]{:S(2)}) copy-start(bf16[2048,512]{1,0:T(8,128)(2,1)} %refs_8_.1) | copy-start | bytes 6291460
  48.7 8.3 %collective-permute-start.13 = (bf16[272,128]{1,0:T(8,128)(2,1)S(1)}, bf16[272,128]{1,0:T(8,128)(2,1)S(1)}, u32[]{:S(2)}, u32[]{:S(2)}) collective-permute-start(bf16[272,128]{1,0:T(8,128)(2,1)S(1)} %get-tuple-element.37), channel_id=1, source_target_pairs={{0,32},{8,40},{16,48},{24,56},{32,64},{40,72},{48,80},{56,88},{64,... | collective-permute-start | bytes 208904 | tf_op jit(solution)/shard_map/ppermute | solution.py:327
  48.8 8.2 %collective-permute-start.14 = (bf16[272,128]{1,0:T(8,128)(2,1)S(1)}, bf16[272,128]{1,0:T(8,128)(2,1)S(1)}, u32[]{:S(2)}, u32[]{:S(2)}) collective-permute-start(bf16[272,128]{1,0:T(8,128)(2,1)S(1)} %get-tuple-element.51), channel_id=1, source_target_pairs={{0,224},{8,232},{16,240},{24,248},{32,0},{40,8},{48,16},{56,24},{6... | collective-permute-start | bytes 208904 | tf_op jit(solution)/shard_map/ppermute | solution.py:327
  51.9 5.6 %collective-permute-start.15 = (bf16[272,128]{1,0:T(8,128)(2,1)S(1)}, bf16[272,128]{1,0:T(8,128)(2,1)S(1)}, u32[]{:S(2)}, u32[]{:S(2)}) collective-permute-start(bf16[272,128]{1,0:T(8,128)(2,1)S(1)} %get-tuple-element.48), channel_id=1, source_target_pairs={{0,64},{8,72},{16,80},{24,88},{32,96},{40,104},{48,112},{56,120},{... | collective-permute-start | bytes 208904 | tf_op jit(solution)/shard_map/ppermute | solution.py:327
  51.9 5.5 %collective-permute-start.16 = (bf16[272,128]{1,0:T(8,128)(2,1)S(1)}, bf16[272,128]{1,0:T(8,128)(2,1)S(1)}, u32[]{:S(2)}, u32[]{:S(2)}) collective-permute-start(bf16[272,128]{1,0:T(8,128)(2,1)S(1)} %get-tuple-element.52), channel_id=1, source_target_pairs={{0,192},{8,200},{16,208},{24,216},{32,224},{40,232},{48,240},{56,2... | collective-permute-start | bytes 208904 | tf_op jit(solution)/shard_map/ppermute | solution.py:327
  57.8 4.7 %collective-permute-start.17 = (bf16[256,128]{1,0:T(8,128)(2,1)S(1)}, bf16[256,128]{1,0:T(8,128)(2,1)S(1)}, u32[]{:S(2)}, u32[]{:S(2)}) collective-permute-start(bf16[256,128]{1,0:T(8,128)(2,1)S(1)} %merge.3), channel_id=1, source_target_pairs={{0,16},{8,24},{16,0},{24,8},{32,48},{40,56},{48,32},{56,40},{64,80... | collective-permute-start | bytes 196616 | tf_op jit(solution)/shard_map/ppermute | solution.py:327
  62.5 7.0 %collective-permute-start.19 = (bf16[512,128]{1,0:T(8,128)(2,1)S(1)}, bf16[512,128]{1,0:T(8,128)(2,1)S(1)}, u32[]{:S(2)}, u32[]{:S(2)}) collective-permute-start(bf16[512,128]{1,0:T(8,128)(2,1)S(1)} %pad_maximum_fusion.refs_0_), channel_id=1, source_target_pairs={{0,192},{8,200},{16,208},{24,216},{32,224},{40,232},{48,240},{56,2... | collective-permute-start | bytes 393224 | tf_op jit(solution)/shard_map/ppermute | solution.py:327
  65.9 5.3 %collective-permute-start.18 = (bf16[512,128]{1,0:T(8,128)(2,1)S(1)}, bf16[512,128]{1,0:T(8,128)(2,1)S(1)}, u32[]{:S(2)}, u32[]{:S(2)}) collective-permute-start(bf16[512,128]{1,0:T(8,128)(2,1)S(1)} %pad_maximum_fusion.refs_0_), channel_id=1, source_target_pairs={{0,224},{8,232},{16,240},{24,248},{32,0},{40,8},{48,16},{56,24},{6... | collective-permute-start | bytes 393224 | tf_op jit(solution)/shard_map/ppermute | solution.py:327
  65.9 7.0 %collective-permute-start.22 = (bf16[512,128]{1,0:T(8,128)(2,1)S(1)}, bf16[512,128]{1,0:T(8,128)(2,1)S(1)}, u32[]{:S(2)}, u32[]{:S(2)}) collective-permute-start(bf16[512,128]{1,0:T(8,128)(2,1)S(1)} %pad_maximum_fusion.refs_0_), channel_id=1, source_target_pairs={{0,64},{8,72},{16,80},{24,88},{32,96},{40,104},{48,112},{56,120},{... | collective-permute-start | bytes 393224 | tf_op jit(solution)/shard_map/ppermute | solution.py:327
  66.0 8.8 %collective-permute-start.24 = (bf16[512,128]{1,0:T(8,128)(2,1)S(1)}, bf16[512,128]{1,0:T(8,128)(2,1)S(1)}, u32[]{:S(2)}, u32[]{:S(2)}) collective-permute-start(bf16[512,128]{1,0:T(8,128)(2,1)S(1)} %pad_maximum_fusion.refs_0_), channel_id=1, source_target_pairs={{0,32},{8,40},{16,48},{24,56},{32,64},{40,72},{48,80},{56,88},{64,... | collective-permute-start | bytes 393224 | tf_op jit(solution)/shard_map/ppermute | solution.py:327
  69.5 6.7 %collective-permute-start.20 = (bf16[512,128]{1,0:T(8,128)(2,1)S(1)}, bf16[512,128]{1,0:T(8,128)(2,1)S(1)}, u32[]{:S(2)}, u32[]{:S(2)}) collective-permute-start(bf16[512,128]{1,0:T(8,128)(2,1)S(1)} %collective-permute-done.19.refs_2_), channel_id=1, source_target_pairs={{0,224},{8,232},{16,240},{24,248},{32,0},{40,8},{48,16},{56,24},{6... | collective-permute-start | bytes 393224 | tf_op jit(solution)/shard_map/ppermute | solution.py:327
  71.1 9.1 %collective-permute-start.21 = (bf16[512,128]{1,0:T(8,128)(2,1)S(1)}, bf16[512,128]{1,0:T(8,128)(2,1)S(1)}, u32[]{:S(2)}, u32[]{:S(2)}) collective-permute-start(bf16[512,128]{1,0:T(8,128)(2,1)S(1)} %collective-permute-done.19.refs_2_), channel_id=1, source_target_pairs={{0,192},{8,200},{16,208},{24,216},{32,224},{40,232},{48,240},{56,2... | collective-permute-start | bytes 393224 | tf_op jit(solution)/shard_map/ppermute | solution.py:327
  72.9 7.6 %collective-permute-start.23 = (bf16[512,128]{1,0:T(8,128)(2,1)S(1)}, bf16[512,128]{1,0:T(8,128)(2,1)S(1)}, u32[]{:S(2)}, u32[]{:S(2)}) collective-permute-start(bf16[512,128]{1,0:T(8,128)(2,1)S(1)} %collective-permute-done.22.refs_6_), channel_id=1, source_target_pairs={{0,32},{8,40},{16,48},{24,56},{32,64},{40,72},{48,80},{56,88},{64,... | collective-permute-start | bytes 393224 | tf_op jit(solution)/shard_map/ppermute | solution.py:327
  93.6 8.6 %collective-permute-start.26 = (bf16[32,512]{1,0:T(8,128)(2,1)S(1)}, bf16[32,512]{1,0:T(8,128)(2,1)S(1)}, u32[]{:S(2)}, u32[]{:S(2)}) collective-permute-start(bf16[32,512]{1,0:T(8,128)(2,1)S(1)} %get-tuple-element.54), channel_id=1, source_target_pairs={{0,8},{8,0},{16,24},{24,16},{32,40},{40,32},{48,56},{56,48},{64,72... | collective-permute-start | bytes 98312 | tf_op jit(solution)/shard_map/ppermute | solution.py:327
where the time goes:
time: 105 us; the launch traced here: 103 us
  starting transfers between devices  48.5 us (46%)
  waiting for transfers between devices  18.5 us (18%)
  Pallas kernels  18.3 us (17%)
  blocking collectives  11.5 us (11%)
  local copies, waits for them, and re-layouts  2.83 us (3%)
  other arithmetic  1.71 us (2%)
  between operations  1.48 us (1%)
    ppermute x27, starting transfers between devices, send(): return lax.ppermute(value, 'ctx', permutation(dz, dx, dc))  48.5 us
    ppermute x27, waiting for transfers between devices, send(): return lax.ppermute(value, 'ctx', permutation(dz, dx, dc))  18.5 us
    all_to_all x1, blocking collectives, on_device(): lax.all_to_all(terms, 'kvh', 0, 0, tiled=True).astype(jnp.float32)  11.5 us
    pallas_call x4, Pallas kernels, flash_second(): pl.pallas_call(functools.partial(second_kernel, offsets, shards, first),...  8.54 us
    pallas_call x3, Pallas kernels, flash_first(): pl.pallas_call(functools.partial(first_kernel, chunks), out_shape=(jax.Sh...  6.48 us
    unnamed x8, local copies, waits for them, and re-layouts  2.74 us
  transfers between devices with their start and end apart: 27, of which 15 were waited for; matrix products, arithmetic and copies ran while one was open for 1% of the time, Pallas kernels for 16%

commit v1 on v0

--- a/solution.py
+++ b/solution.py
@@ -13,60 +13,73 @@
 LOG2E = 1.4426950408889634
 HD = 128
 STAT = 16
+CTX = ("z", "x", "c")
 VMEM = pl.BlockSpec(memory_space=pltpu.VMEM)
 HBM = pl.BlockSpec(memory_space=pltpu.HBM)
 
 
-def prepare_kernel(q_hbm, k_hbm, v_hbm, fresh, cosine, sine, q_out, pack_out, q_in, turned, sems):
-    n = k_hbm.shape[0]
-    piece = n // 4
-    copies = [pltpu.make_async_copy(q_hbm, q_in, sems.at[0])]
-    for i in range(8):
-        source = (k_hbm, v_hbm)[i // 4].at[i % 4 * piece : (i % 4 + 1) * piece]
-        target = pack_out.at[i * piece : (i + 1) * piece]
-        copies.append(pltpu.make_async_copy(source, target, sems.at[1 + i]))
-    for copy in copies:
-        copy.start()
+def rotate_kernel(q_ref, cosine, sine, q_out, turned):
+    tokens, heads, width = q_ref.shape
     cos, sin = cosine[...], sine[...]
-    new_k = fresh[0:16, :].astype(jnp.float32)
-    new_k = new_k * cos + pltpu.roll(new_k, HD // 2, 1) * sin
-    pack_out[2 * n : 2 * n + 16, :] = new_k.astype(jnp.bfloat16)
-    pack_out[2 * n + 16 : 2 * n + NOTE, :] = fresh[16:NOTE, :]
-    copies[0].wait()
-    tokens, heads, width = q_in.shape
-    old = q_in[...].astype(jnp.float32)
+    old = q_ref[...].astype(jnp.float32)
     swapped = pltpu.roll(old.reshape(tokens * heads, width), HD // 2, 1).reshape(old.shape)
     turned[...] = old * cos[:, None, :] + swapped * sin[:, None, :]
     for h in range(heads):
         q_out[tokens * h : tokens * (h + 1), :] = turned[:, h, :].astype(jnp.bfloat16)
-    for copy in copies[1:]:
+
+
+def rotate(queries, cosine, sine):
+    tokens, heads, width = queries.shape
+    return pl.pallas_call(
+        rotate_kernel,
+        out_shape=jax.ShapeDtypeStruct((tokens * heads, width), jnp.bfloat16),
+        in_specs=[VMEM] * 3,
+        out_specs=VMEM,
+        scratch_shapes=[pltpu.VMEM(queries.shape, jnp.float32)],
+        compiler_params=pltpu.CompilerParams(vmem_limit_bytes=12 << 20),
+        cost_estimate=pl.CostEstimate(flops=1 << 18, bytes_accessed=1 << 17, transcendentals=0),
+        name="rotate",
+    )(queries, cosine, sine)
+
+
+def pack_kernel(k_hbm, v_hbm, fresh, cosine, sine, pack_out, sems):
+    n = k_hbm.shape[0]
+    piece = n // 4
+    copies = []
+    for i in range(8):
+        source = (k_hbm, v_hbm)[i // 4].at[i % 4 * piece : (i % 4 + 1) * piece]
+        target = pack_out.at[i * piece : (i + 1) * piece]
+        copies.append(pltpu.make_async_copy(source, target, sems.at[i]))
+    for copy in copies:
+        copy.start()
+    new_k = fresh[0:16, :].astype(jnp.float32)
+    new_k = new_k * cosine[...] + pltpu.roll(new_k, HD // 2, 1) * sine[...]
+    pack_out[2 * n : 2 * n + 16, :] = new_k.astype(jnp.bfloat16)
+    pack_out[2 * n + 16 : 2 * n + NOTE, :] = fresh[16:NOTE, :]
+    for copy in copies:
         copy.wait()
 
 
-def prepare(queries, keys, values, fresh, positions):
-    tokens, heads, width = queries.shape
+def pack_up(keys, values, fresh, cosine, sine):
+    n, width = keys.shape
+    return pl.pallas_call(
+        pack_kernel,
+        out_shape=jax.ShapeDtypeStruct((2 * n + NOTE, width), jnp.bfloat16),
+        in_specs=[HBM] * 2 + [VMEM] * 3,
+        out_specs=VMEM,
+        scratch_shapes=[pltpu.SemaphoreType.DMA((8,))],
+        compiler_params=pltpu.CompilerParams(vmem_limit_bytes=12 << 20),
+        cost_estimate=pl.CostEstimate(flops=1 << 18, bytes_accessed=1 << 20, transcendentals=0),
+        name="pack_up",
+    )(keys, values, fresh, cosine, sine)
+
+
+def turning(positions, width):
     steps_index = jnp.arange(width // 2, dtype=jnp.float32)
     inverse = jnp.exp(steps_index * (-2.0 * math.log(ROPE_BASE) / width))
     angles = positions[:, None] * jnp.concatenate([inverse, inverse])[None, :]
     sign = jnp.where(jnp.arange(width) < width // 2, -1.0, 1.0).astype(jnp.float32)
-    n = keys.shape[0]
-    return pl.pallas_call(
-        prepare_kernel,
-        out_shape=(
-            jax.ShapeDtypeStruct((tokens * heads, width), jnp.bfloat16),
-            jax.ShapeDtypeStruct((2 * n + NOTE, width), jnp.bfloat16),
-        ),
-        in_specs=[HBM] * 3 + [VMEM] * 3,
-        out_specs=(VMEM, VMEM),
-        scratch_shapes=[
-            pltpu.VMEM(queries.shape, jnp.bfloat16),
-            pltpu.VMEM(queries.shape, jnp.float32),
-            pltpu.SemaphoreType.DMA((9,)),
-        ],
-        compiler_params=pltpu.CompilerParams(vmem_limit_bytes=12 << 20),
-        cost_estimate=pl.CostEstimate(flops=1 << 18, bytes_accessed=1 << 20, transcendentals=0),
-        name="prepare",
-    )(queries, keys, values, fresh, jnp.cos(angles), jnp.sin(angles) * sign)
+    return jnp.cos(angles), jnp.sin(angles) * sign
 
 
 def dot_nt(a, b):
@@ -160,8 +173,7 @@
 
 
 def place():
-    me = lax.axis_index("ctx")
-    return me >> 2, (me >> 1) & 1, me & 1
+    return lax.axis_index("z"), lax.axis_index("x"), lax.axis_index("c")
 
 
 def second_kernel(offsets, shards, first, *refs):
@@ -268,7 +280,7 @@
 
 def project_kernel(chunks, *refs):
     pair_refs, (w_own, w_core, out_ref, left_ref) = refs[:chunks], refs[chunks:]
-    my_z, my_x, _ = place()
+    my_z, my_x, my_c = place()
     heads = left_ref.shape[3] // HD
     for i in range(chunks):
         home = lax.rem(my_z + i, chunks)
@@ -279,12 +291,9 @@
                     first : first + 16, :
                 ]
     left = left_ref[...].reshape(chunks * 32, heads * HD)
-    width = w_own.shape[1]
     for k, w in enumerate((w_own, w_core)):
         terms = jnp.dot(left, w[...], preferred_element_type=jnp.float32)
-        out_ref[:, :, k * width : (k + 1) * width] = terms.astype(jnp.bfloat16).reshape(
-            chunks, 32, width
-        )
+        out_ref[my_c ^ k] = terms.astype(jnp.bfloat16).reshape(chunks, 32, w.shape[1])
 
 
 def project(pairs, w_own, w_core):
@@ -292,7 +301,7 @@
     depth, width = w_own.shape
     return pl.pallas_call(
         functools.partial(project_kernel, chunks),
-        out_shape=jax.ShapeDtypeStruct((chunks, 32, 2 * width), jnp.bfloat16),
+        out_shape=jax.ShapeDtypeStruct((2, chunks, 32, width), jnp.bfloat16),
         in_specs=[VMEM] * (chunks + 2),
         out_specs=VMEM,
         scratch_shapes=[pltpu.VMEM((chunks, 2, 16, depth), jnp.bfloat16)],
@@ -304,14 +313,35 @@
     )(*pairs, w_own, w_core)
 
 
+def total_kernel(in_ref, out_ref):
+    shards = in_ref.shape[0] // 2
+    for c in range(2):
+        acc = in_ref[c * shards].astype(jnp.float32)
+        for g in range(1, shards):
+            acc = acc + in_ref[c * shards + g].astype(jnp.float32)
+        for x in range(2):
+            first = (2 * x + c) * 16
+            out_ref[first : first + 16, :] = acc[16 * x : 16 * x + 16].astype(jnp.bfloat16)
+
+
+def total(got):
+    return pl.pallas_call(
+        total_kernel,
+        out_shape=jax.ShapeDtypeStruct((64, got.shape[2]), jnp.bfloat16),
+        in_specs=[VMEM],
+        out_specs=VMEM,
+        compiler_params=pltpu.CompilerParams(vmem_limit_bytes=8 << 20),
+        cost_estimate=pl.CostEstimate(flops=1 << 18, bytes_accessed=1 << 19, transcendentals=0),
+        name="total",
+    )(got)
+
+
 def on_device(
     queries, cache_keys, cache_values, new_keys, new_values, fill_rows, turn_start, out_weight
 ):
     tok_dev, group_size, head_width = queries.shape
-    ctx_count = lax.axis_size("ctx")
-    shards = ctx_count // 4
-    me = lax.axis_index("ctx")
-    my_z, my_x, my_c = me // 4, (me // 2) % 2, me % 2
+    shards = lax.axis_size("z")
+    me = lax.axis_index(CTX)
     cache_rows = cache_keys.shape[0]
 
     def permutation(dz, dx, dc):
@@ -324,7 +354,7 @@
         ]
 
     def send(value, dz=0, dx=0, dc=0):
-        return lax.ppermute(value, "ctx", permutation(dz, dx, dc))
+        return lax.ppermute(value, CTX, permutation(dz, dx, dc))
 
     def after(value, *others):
         return lax.optimization_barrier((value,) + others)[0]
@@ -332,7 +362,8 @@
     positions = (turn_start[0] + me * tok_dev + jnp.arange(tok_dev, dtype=jnp.int32)).astype(
         jnp.float32
     )
-    q = {}
+    cosine, sine = turning(positions, head_width)
+    q = {0: rotate(queries, cosine, sine)}
     fresh = jnp.concatenate(
         [
             new_keys.reshape(tok_dev, head_width),
@@ -341,26 +372,25 @@
         ],
         axis=0,
     )
-    q[0], pack = prepare(
-        queries,
+    pack = pack_up(
         cache_keys.reshape(cache_rows, head_width),
         cache_values.reshape(cache_rows, head_width),
-        fresh,
-        positions,
+        after(fresh, q[0]),
+        cosine,
+        sine,
     )
-    pack_x, pack_c = send(pack, dx=1), send(pack, dc=1)
+    pack_x = send(pack, dx=1)
     for d in (1, -1, 2, -2):
         q[d] = send(q[0], dz=-d)
     here, close, wide, outer = (0,), (1, -1), (2, -2), (3, -3, 4)
+    arrived = (q[1], q[-1], q[2], q[-2])
+    pack_c, pack_xc = send(after(pack, *arrived), dc=1), send(after(pack_x, *arrived), dc=1)
+    up, down = after(q[2], *arrived), after(q[-2], *arrived)
+    q[3], q[-3], q[4] = send(up, dz=-1), send(down, dz=1), send(up, dz=-2)
     state = {here: flash_first([q[0]], (pack, pack_c))}
-    arrived = (q[1], q[-1], state[here][1])
-    pack_x = after(pack_x, q[2], q[-2], *arrived)
-    pack_xc = send(pack_x, dc=1)
-    up, down = after(q[2], q[-2], *arrived), after(q[-2], q[2], *arrived)
-    q[3], q[-3], q[4] = send(up, dz=-1), send(down, dz=1), send(up, dz=-2)
     both = flash_first([q[d] for d in close + wide], (pack, pack_c))
     state[close], state[wide] = both, both
-    q[-3] = after(q[-3], both[1])
+    q[-3] = after(q[-3], both[1], state[here][1])
     state[outer] = flash_first([q[d] for d in outer], (pack, pack_c))
     packs = (pack, pack_c, pack_x, pack_xc)
 
@@ -390,35 +420,17 @@
     pair[3], pair[-3], pair[4] = send(pair[2], dz=-1), send(pair[-2], dz=1), send(pair[2], dz=-2)
     w_core = send(out_weight, dc=1)
     terms = project([pair[d if d <= 4 else d - 8] for d in range(8)], out_weight, w_core)
-    summed = (
-        lax.all_to_all(terms, "kvh", 0, 0, tiled=True)
-        .astype(jnp.float32)
-        .sum(axis=0)
-        .astype(jnp.bfloat16)
+    width = out_weight.shape[1]
+    terms = terms.reshape(2 * shards, 2 * tok_dev, width)
+    got = lax.all_to_all(terms, ("c", "kvh"), 0, 0, tiled=True)
+    return total(got)
+
+
+def solution(mesh):
+    shape = (mesh.shape["ctx"] // 4, 2, 2, mesh.shape["kvh"])
+    fine = jax.sharding.Mesh(mesh.devices.reshape(shape), CTX + ("kvh",))
+    split = P(CTX, "kvh", None)
+    in_specs = (split, split, split, split, split, P(CTX), P(), P("kvh", CTX))
+    return jax.shard_map(
+        on_device, mesh=fine, in_specs=in_specs, out_specs=P("kvh", CTX), check_vma=False
     )
-    width = out_weight.shape[1]
-    mine = summed[:, :width].reshape(2, 1, tok_dev, width)
-    other = send(summed[:, width:], dc=1).reshape(2, 1, tok_dev, width)
-    ordered = jnp.where(
-        my_c == 0,
-        jnp.concatenate([mine, other], axis=1),
-        jnp.concatenate([other, mine], axis=1),
-    )
-    return ordered.reshape(4 * tok_dev, width)
-
-
-def solution(mesh):
-    in_specs = (
-        P("ctx", "kvh", None),
-        P("ctx", "kvh", None),
-        P("ctx", "kvh", None),
-        P("ctx", "kvh", None),
-        P("ctx", "kvh", None),
-        P("ctx"),
-        P(),
-        P("kvh", "ctx"),
-    )
-    out_specs = P("kvh", "ctx")
-    return jax.shard_map(
-        on_device, mesh=mesh, in_specs=in_specs, out_specs=out_specs, check_vma=False
-    )

time: 105 us -> 104 us (level); the launches traced: 103 us -> 103 us
  blocking collectives: 11.5 us -> 21.2 us
  starting transfers between devices: 48.5 us -> 41.4 us
  waiting for transfers between devices: 18.5 us -> 16.3 us
    all_to_all x1, blocking collectives: 11.5 us -> 21.2 us  [on_device(): got = lax.all_to_all(terms, ('c', 'kvh'), 0, 0, tiled=True)]
    ppermute x27 -> x26, starting transfers between devices: 48.5 us -> 41.4 us  [send(): return lax.ppermute(value, CTX, permutation(dz, dx, dc))]
    ppermute x27 -> x26, waiting for transfers between devices: 18.5 us -> 16.3 us  [send(): return lax.ppermute(value, CTX, permutation(dz, dx, dc))]
  transfers between devices with their start and end apart: 27 -> 26, of which waited for: 15 -> 12; matrix products, arithmetic and copies ran while one was open for 1% -> 1% of each run, Pallas kernels for 16% -> 16%
where the time goes in v1:
time: 104 us; the launch traced here: 103 us
  starting transfers between devices  41.4 us (40%)
  blocking collectives  21.2 us (20%)
  Pallas kernels  18.8 us (18%)
  waiting for transfers between devices  16.3 us (16%)
  local copies, waits for them, and re-layouts  2.83 us (3%)
  between operations  1.5 us (1%)
    ppermute x26, starting transfers between devices, send(): return lax.ppermute(value, CTX, permutation(dz, dx, dc))  41.4 us
    all_to_all x1, blocking collectives, on_device(): got = lax.all_to_all(terms, ('c', 'kvh'), 0, 0, tiled=True)  21.2 us
    ppermute x26, waiting for transfers between devices, send(): return lax.ppermute(value, CTX, permutation(dz, dx, dc))  16.3 us
    pallas_call x4, Pallas kernels, flash_second(): pl.pallas_call(functools.partial(second_kernel, offsets, shards, first),...  8.63 us
    pallas_call x3, Pallas kernels, flash_first(): pl.pallas_call(functools.partial(first_kernel, chunks), out_shape=(jax.Sh...  6.3 us
    unnamed x8, local copies, waits for them, and re-layouts  2.75 us
  transfers between devices with their start and end apart: 26, of which 12 were waited for; matrix products, arithmetic and copies ran while one was open for 1% of the time, Pallas kernels for 16%

profile of v1, /device:TPU:1, one launch (start us, length us, event | category | flops | bytes accessed | tf_op | source)
XLA Modules:
  0.0 103.0 jit_solution(8334574172211198593)
XLA Ops:
  0.0 3.2 %collective-permute-start.25 = (bf16[2048,512]{1,0:T(8,128)(2,1)}, bf16[2048,512]{1,0:T(8,128)(2,1)S(1)}, u32[]{:S(2)}, u32[]{:S(2)}) collective-permute-start(bf16[2048,512]{1,0:T(8,128)(2,1)} %refs_8_.1), channel_id=1, source_target_pairs={{0,8},{8,0},{16,24},{24,16},{32,40},{40,32},{48,56},{56,48},{64,72... | collective-permute-start | bytes 6291464 | tf_op jit(solution)/shard_map/ppermute | solution.py:357
  3.3 0.1 compare_select_fusion
  4.0 0.1 fusion
  4.1 0.0 copy-start.3
  4.1 0.8 copy-done.3
  5.0 0.2 rotate.1.refs_0_
  5.9 0.1 pad.4.clone
  6.0 0.8 maximum_maximum_fusion.fresh
  6.7 1.0 copy-done.1
  7.7 0.9 copy-done.2
  8.6 0.8 pack_up.1.refs_4_.refs_1_.refs_3_.refs_5_
  9.4 1.1 %collective-permute-start.5 = (bf16[2096,128]{1,0:T(8,128)(2,1)S(1)}, bf16[2096,128]{1,0:T(8,128)(2,1)S(1)}, u32[]{:S(2)}, u32[]{:S(2)}) collective-permute-start(bf16[2096,128]{1,0:T(8,128)(2,1)S(1)} %pack_up.1.refs_4_.refs_1_.refs_3_.refs_5_), channel_id=1, source_target_pairs={{0,16},{8,24},{16,0},{24,8},{32,48},{40,56},{48,32},{56,40},{64,80... | collective-permute-start | bytes 1609736 | tf_op jit(solution)/shard_map/ppermute | solution.py:357
  10.5 6.0 %collective-permute-start = (bf16[256,128]{1,0:T(8,128)(2,1)S(1)}, bf16[256,128]{1,0:T(8,128)(2,1)S(1)}, u32[]{:S(2)}, u32[]{:S(2)}) collective-permute-start(bf16[256,128]{1,0:T(8,128)(2,1)S(1)} %rotate.1.refs_0_), channel_id=1, source_target_pairs={{0,192},{8,200},{16,208},{24,216},{32,224},{40,232},{48,240},{56,2... | collective-permute-start | bytes 196616 | tf_op jit(solution)/shard_map/ppermute | solution.py:357
  16.6 3.1 %collective-permute-start.2 = (bf16[256,128]{1,0:T(8,128)(2,1)S(1)}, bf16[256,128]{1,0:T(8,128)(2,1)S(1)}, u32[]{:S(2)}, u32[]{:S(2)}) collective-permute-start(bf16[256,128]{1,0:T(8,128)(2,1)S(1)} %rotate.1.refs_0_), channel_id=1, source_target_pairs={{0,224},{8,232},{16,240},{24,248},{32,0},{40,8},{48,16},{56,24},{6... | collective-permute-start | bytes 196616 | tf_op jit(solution)/shard_map/ppermute | solution.py:357
  19.7 0.0 collective-permute-start.3
  19.7 2.6 %collective-permute-done.1.refs_3_.refs_1_ = bf16[256,128]{1,0:T(8,128)(2,1)S(1)} collective-permute-done((bf16[256,128]{1,0:T(8,128)(2,1)S(1)}, bf16[256,128]{1,0:T(8,128)(2,1)S(1)}, u32[]{:S(2)}, u32[]{:S(2)}) %collective-permute-start.1) | collective-permute-done | bytes 65568 | tf_op jit(solution)/shard_map/ppermute | solution.py:357
  22.3 2.1 %collective-permute-done.3.refs_1_ = bf16[256,128]{1,0:T(8,128)(2,1)S(1)} collective-permute-done((bf16[256,128]{1,0:T(8,128)(2,1)S(1)}, bf16[256,128]{1,0:T(8,128)(2,1)S(1)}, u32[]{:S(2)}, u32[]{:S(2)}) %collective-permute-start.3) | collective-permute-done | bytes 65568 | tf_op jit(solution)/shard_map/ppermute | solution.py:357
  24.4 1.9 %collective-permute-start.4 = (bf16[2096,128]{1,0:T(8,128)(2,1)S(1)}, bf16[2096,128]{1,0:T(8,128)(2,1)S(1)}, u32[]{:S(2)}, u32[]{:S(2)}) collective-permute-start(bf16[2096,128]{1,0:T(8,128)(2,1)S(1)} %pack_up.1.refs_4_.refs_1_.refs_3_.refs_5_), channel_id=1, source_target_pairs={{0,8},{8,0},{16,24},{24,16},{32,40},{40,32},{48,56},{56,48},{64,72... | collective-permute-start | bytes 1609736 | tf_op jit(solution)/shard_map/ppermute | solution.py:357
  26.3 0.0 collective-permute-done.5.refs_6_.refs_7_.refs_5_
  26.3 0.0 collective-permute-start.6
  26.3 3.2 %collective-permute-start.7 = (bf16[256,128]{1,0:T(8,128)(2,1)S(1)}, bf16[256,128]{1,0:T(8,128)(2,1)S(1)}, u32[]{:S(2)}, u32[]{:S(2)}) collective-permute-start(bf16[256,128]{1,0:T(8,128)(2,1)S(1)} %collective-permute-done.refs_2_.refs_0_), channel_id=1, source_target_pairs={{0,224},{8,232},{16,240},{24,248},{32,0},{40,8},{48,16},{56,24},{6... | collective-permute-start | bytes 196616 | tf_op jit(solution)/shard_map/ppermute | solution.py:357
  29.5 1.2 %collective-permute-start.9 = (bf16[256,128]{1,0:T(8,128)(2,1)S(1)}, bf16[256,128]{1,0:T(8,128)(2,1)S(1)}, u32[]{:S(2)}, u32[]{:S(2)}) collective-permute-start(bf16[256,128]{1,0:T(8,128)(2,1)S(1)} %collective-permute-done.refs_2_.refs_0_), channel_id=1, source_target_pairs={{0,192},{8,200},{16,208},{24,216},{32,224},{40,232},{48,240},{56,2... | collective-permute-start | bytes 196616 | tf_op jit(solution)/shard_map/ppermute | solution.py:357
  30.7 0.0 collective-permute-done.4.refs_5_.refs_2_.refs_4_.refs_6_
  30.7 0.7 collective-permute-start.8
  31.4 2.9 %flash_first.3 = (f32[4,256,256]{2,1,0:T(8,128)S(1)}, f32[4,256,128]{2,1,0:T(8,128)S(1)}) custom-call(bf16[256,128]{1,0:T(8,128)(2,1)S(1)} %collective-permute-done.2.refs_0_, bf16[256,128]{1,0:T(8,128)(2,1)S(1)} %collective-permute-done.3.refs_1_, bf16[256,128]{1,0:T(8,128)(2,1)S(1)} %collective-permute-done.refs_2_.refs_0_, ...), custom_call_target="tpu_custom_call" | custom-call | flops 2147483648 | bytes 1048576 | tf_op jit(solution)/shard_map/flash_first/pallas_call | solution.py:148
  34.3 1.0 flash_first.4
  35.3 0.0 collective-permute-done.7.refs_0_
  35.3 0.0 collective-permute-done.9.refs_2_
  35.3 2.4 %flash_first.5 = (f32[3,256,256]{2,1,0:T(8,128)S(1)}, f32[3,256,128]{2,1,0:T(8,128)S(1)}) custom-call(bf16[256,128]{1,0:T(8,128)(2,1)S(1)} %collective-permute-done.7.refs_0_, bf16[256,128]{1,0:T(8,128)(2,1)S(1)} %collective-permute-done.8.refs_1_, bf16[256,128]{1,0:T(8,128)(2,1)S(1)} %collective-permute-done.9.refs_2_, ...), custom_call_target="tpu_custom_call" | custom-call | flops 1610612736 | bytes 1048576 | tf_op jit(solution)/shard_map/flash_first/pallas_call | solution.py:148
  37.7 0.0 collective-permute-done.6.refs_7_.refs_8_.refs_6_
  37.8 3.0 %flash_second.6 = (bf16[272,128]{1,0:T(8,128)(2,1)S(1)}, bf16[272,128]{1,0:T(8,128)(2,1)S(1)}, bf16[272,128]{1,0:T(8,128)(2,1)S(1)}) custom-call(bf16[256,128]{1,0:T(8,128)(2,1)S(1)} %collective-permute-done.7.refs_0_, bf16[256,128]{1,0:T(8,128)(2,1)S(1)} %collective-permute-done.8.refs_1_, bf16[256,128]{1,0:T(8,128)(2,1)S(1)} %collective-permute-done.9.refs_2_, ...), custom_call_target="tpu_custom_call" | custom-call | flops 1048576 | bytes 65536 | tf_op jit(solution)/shard_map/flash_second/pallas_call | solution.py:230
  40.8 0.8 collective-permute-start.10
  41.6 0.6 collective-permute-start.11
  42.2 1.9 %collective-permute-start.12 = (bf16[272,128]{1,0:T(8,128)(2,1)S(1)}, bf16[272,128]{1,0:T(8,128)(2,1)S(1)}, u32[]{:S(2)}, u32[]{:S(2)}) collective-permute-start(bf16[272,128]{1,0:T(8,128)(2,1)S(1)} %get-tuple-element.47), channel_id=1, source_target_pairs={{0,224},{8,232},{16,240},{24,248},{32,0},{40,8},{48,16},{56,24},{6... | collective-permute-start | bytes 208904 | tf_op jit(solution)/shard_map/ppermute | solution.py:357
  44.1 2.0 %flash_second.4 = (bf16[272,128]{1,0:T(8,128)(2,1)S(1)}, bf16[272,128]{1,0:T(8,128)(2,1)S(1)}) custom-call(bf16[256,128]{1,0:T(8,128)(2,1)S(1)} %collective-permute-done.refs_2_.refs_0_, bf16[256,128]{1,0:T(8,128)(2,1)S(1)} %collective-permute-done.1.refs_3_.refs_1_, f32[4,256,256]{2,1,0:T(8,128)S(1)} %get-tuple-element.31.refs_2_, ...), custom_call_target="tpu_custom_call" | custom-call | flops 1048576 | bytes 65536 | tf_op jit(solution)/shard_map/flash_second/pallas_call | solution.py:230
  46.1 2.0 %flash_second.5 = (bf16[272,128]{1,0:T(8,128)(2,1)S(1)}, bf16[272,128]{1,0:T(8,128)(2,1)S(1)}) custom-call(bf16[256,128]{1,0:T(8,128)(2,1)S(1)} %collective-permute-done.2.refs_0_, bf16[256,128]{1,0:T(8,128)(2,1)S(1)} %collective-permute-done.3.refs_1_, f32[4,256,256]{2,1,0:T(8,128)S(1)} %get-tuple-element.31.refs_2_, ...), custom_call_target="tpu_custom_call" | custom-call | flops 1048576 | bytes 65536 | tf_op jit(solution)/shard_map/flash_second/pallas_call | solution.py:230
  48.2 0.0 copy-start
  48.2 0.1 collective-permute-start.13
  48.3 2.7 %collective-permute-start.14 = (bf16[272,128]{1,0:T(8,128)(2,1)S(1)}, bf16[272,128]{1,0:T(8,128)(2,1)S(1)}, u32[]{:S(2)}, u32[]{:S(2)}) collective-permute-start(bf16[272,128]{1,0:T(8,128)(2,1)S(1)} %get-tuple-element.51), channel_id=1, source_target_pairs={{0,224},{8,232},{16,240},{24,248},{32,0},{40,8},{48,16},{56,24},{6... | collective-permute-start | bytes 208904 | tf_op jit(solution)/shard_map/ppermute | solution.py:357
  50.9 0.4 merge.2
  51.4 0.1 collective-permute-start.15
  51.5 3.6 %collective-permute-start.16 = (bf16[272,128]{1,0:T(8,128)(2,1)S(1)}, bf16[272,128]{1,0:T(8,128)(2,1)S(1)}, u32[]{:S(2)}, u32[]{:S(2)}) collective-permute-start(bf16[272,128]{1,0:T(8,128)(2,1)S(1)} %get-tuple-element.52), channel_id=1, source_target_pairs={{0,192},{8,200},{16,208},{24,216},{32,224},{40,232},{48,240},{56,2... | collective-permute-start | bytes 208904 | tf_op jit(solution)/shard_map/ppermute | solution.py:357
  55.0 1.5 %flash_second.7.refs_0_ = bf16[272,128]{1,0:T(8,128)(2,1)S(1)} custom-call(bf16[256,128]{1,0:T(8,128)(2,1)S(1)} %rotate.1.refs_0_, f32[1,256,256]{2,1,0:T(8,128)S(1)} %get-tuple-element.50.refs_1_, f32[1,256,128]{2,1,0:T(8,128)S(1)} %get-tuple-element.40.refs_2_, bf16[2096,128]{1,0:T(8,128)(2,1)S(1)} %pack_up.1.refs_4_.refs_1_.refs_3_.refs_5_, ...), custom_call_target="tpu_custom_call" | custom-call | flops 1048576 | bytes 65536 | tf_op jit(solution)/shard_map/flash_second/pallas_call | solution.py:230
  56.5 0.2 collective-permute-done.15.refs_3_
  56.8 0.6 collective-permute-done.16.refs_4_
  57.4 0.3 merge.3
  57.7 2.8 %collective-permute-start.17 = (bf16[256,128]{1,0:T(8,128)(2,1)S(1)}, bf16[256,128]{1,0:T(8,128)(2,1)S(1)}, u32[]{:S(2)}, u32[]{:S(2)}) collective-permute-start(bf16[256,128]{1,0:T(8,128)(2,1)S(1)} %merge.3), channel_id=1, source_target_pairs={{0,16},{8,24},{16,0},{24,8},{32,48},{40,56},{48,32},{56,40},{64,80... | collective-permute-start | bytes 196616 | tf_op jit(solution)/shard_map/ppermute | solution.py:357
  60.6 1.9 %collective-permute-done.17 = bf16[256,128]{1,0:T(8,128)(2,1)S(1)} collective-permute-done((bf16[256,128]{1,0:T(8,128)(2,1)S(1)}, bf16[256,128]{1,0:T(8,128)(2,1)S(1)}, u32[]{:S(2)}, u32[]{:S(2)}) %collective-permute-start.17) | collective-permute-done | bytes 65568 | tf_op jit(solution)/shard_map/ppermute | solution.py:357
  62.4 3.0 %collective-permute-start.19 = (bf16[512,128]{1,0:T(8,128)(2,1)S(1)}, bf16[512,128]{1,0:T(8,128)(2,1)S(1)}, u32[]{:S(2)}, u32[]{:S(2)}) collective-permute-start(bf16[512,128]{1,0:T(8,128)(2,1)S(1)} %pad_maximum_fusion.refs_0_), channel_id=1, source_target_pairs={{0,192},{8,200},{16,208},{24,216},{32,224},{40,232},{48,240},{56,2... | collective-permute-start | bytes 393224 | tf_op jit(solution)/shard_map/ppermute | solution.py:357
  65.5 0.4 collective-permute-start.22
  65.8 1.4 %collective-permute-start.24 = (bf16[512,128]{1,0:T(8,128)(2,1)S(1)}, bf16[512,128]{1,0:T(8,128)(2,1)S(1)}, u32[]{:S(2)}, u32[]{:S(2)}) collective-permute-start(bf16[512,128]{1,0:T(8,128)(2,1)S(1)} %pad_maximum_fusion.refs_0_), channel_id=1, source_target_pairs={{0,32},{8,40},{16,48},{24,56},{32,64},{40,72},{48,80},{56,88},{64,... | collective-permute-start | bytes 393224 | tf_op jit(solution)/shard_map/ppermute | solution.py:357
  67.2 1.6 %collective-permute-done.19.refs_2_ = bf16[512,128]{1,0:T(8,128)(2,1)S(1)} collective-permute-done((bf16[512,128]{1,0:T(8,128)(2,1)S(1)}, bf16[512,128]{1,0:T(8,128)(2,1)S(1)}, u32[]{:S(2)}, u32[]{:S(2)}) %collective-permute-start.19) | collective-permute-done | bytes 131104 | tf_op jit(solution)/shard_map/ppermute | solution.py:357
  68.9 0.5 collective-permute-start.20
  69.4 0.8 collective-permute-done.18.refs_1_
  70.2 1.3 %collective-permute-start.21 = (bf16[512,128]{1,0:T(8,128)(2,1)S(1)}, bf16[512,128]{1,0:T(8,128)(2,1)S(1)}, u32[]{:S(2)}, u32[]{:S(2)}) collective-permute-start(bf16[512,128]{1,0:T(8,128)(2,1)S(1)} %collective-permute-done.19.refs_2_), channel_id=1, source_target_pairs={{0,192},{8,200},{16,208},{24,216},{32,224},{40,232},{48,240},{56,2... | collective-permute-start | bytes 393224 | tf_op jit(solution)/shard_map/ppermute | solution.py:357
  71.5 0.7 collective-permute-done.22.refs_6_
  72.1 1.9 %collective-permute-start.23 = (bf16[512,128]{1,0:T(8,128)(2,1)S(1)}, bf16[512,128]{1,0:T(8,128)(2,1)S(1)}, u32[]{:S(2)}, u32[]{:S(2)}) collective-permute-start(bf16[512,128]{1,0:T(8,128)(2,1)S(1)} %collective-permute-done.22.refs_6_), channel_id=1, source_target_pairs={{0,32},{8,40},{16,48},{24,56},{32,64},{40,72},{48,80},{56,88},{64,... | collective-permute-start | bytes 393224 | tf_op jit(solution)/shard_map/ppermute | solution.py:357
  74.1 0.2 collective-permute-done.24.refs_7_
  74.2 1.1 %collective-permute-done.20.refs_3_ = bf16[512,128]{1,0:T(8,128)(2,1)S(1)} collective-permute-done((bf16[512,128]{1,0:T(8,128)(2,1)S(1)}, bf16[512,128]{1,0:T(8,128)(2,1)S(1)}, u32[]{:S(2)}, u32[]{:S(2)}) %collective-permute-start.20) | collective-permute-done | bytes 131104 | tf_op jit(solution)/shard_map/ppermute | solution.py:357
  75.4 3.6 %collective-permute-done.21.refs_4_ = bf16[512,128]{1,0:T(8,128)(2,1)S(1)} collective-permute-done((bf16[512,128]{1,0:T(8,128)(2,1)S(1)}, bf16[512,128]{1,0:T(8,128)(2,1)S(1)}, u32[]{:S(2)}, u32[]{:S(2)}) %collective-permute-start.21) | collective-permute-done | bytes 131104 | tf_op jit(solution)/shard_map/ppermute | solution.py:357
  79.0 0.7 collective-permute-done.23.refs_5_
  79.7 1.4 %project.1 = bf16[2,8,32,512]{3,2,1,0:T(8,128)(2,1)S(1)} custom-call(bf16[512,128]{1,0:T(8,128)(2,1)S(1)} %pad_maximum_fusion.refs_0_, bf16[512,128]{1,0:T(8,128)(2,1)S(1)} %collective-permute-done.18.refs_1_, bf16[512,128]{1,0:T(8,128)(2,1)S(1)} %collective-permute-done.19.refs_2_, bf16[512,128]{1,0:T(8,128)(2,1)S(1)} %collective-permute-done.20.refs_3_, ...), custom_call_target="tpu_custom_call" | custom-call | flops 1073741824 | bytes 6291456 | tf_op jit(solution)/shard_map/project/pallas_call | solution.py:302
  81.1 21.2 %all_to_all.5.in_ref = bf16[16,32,512]{2,1,0:T(8,128)(2,1)S(1)} all-to-all(bf16[16,32,512]{2,1,0:T(8,128)(2,1)S(1)} %bitcast.8), channel_id=1, replica_groups=mesh['z'=8,'x'=2,'c'=2,'kvh'=8] {'c','kvh'}, dimensions={0} | all-to-all | bytes 1048576 | tf_op jit(solution)/shard_map/all_to_all | solution.py:425
  102.3 0.7 total.1
  (18 shorter events, 0.1 us)
Async XLA Ops:
  0.0 79.7 %collective-permute-start.25 = (bf16[2048,512]{1,0:T(8,128)(2,1)}, bf16[2048,512]{1,0:T(8,128)(2,1)S(1)}, u32[]{:S(2)}, u32[]{:S(2)}) collective-permute-start(bf16[2048,512]{1,0:T(8,128)(2,1)} %refs_8_.1), channel_id=1, source_target_pairs={{0,8},{8,0},{16,24},{24,16},{32,40},{40,32},{48,56},{56,48},{64,72... | collective-permute-start | bytes 6291464 | tf_op jit(solution)/shard_map/ppermute | solution.py:357
  4.1 0.8 copy-start.3
  6.7 1.0 copy-start.1
  7.7 0.9 copy-start.2
  9.4 16.9 %collective-permute-start.5 = (bf16[2096,128]{1,0:T(8,128)(2,1)S(1)}, bf16[2096,128]{1,0:T(8,128)(2,1)S(1)}, u32[]{:S(2)}, u32[]{:S(2)}) collective-permute-start(bf16[2096,128]{1,0:T(8,128)(2,1)S(1)} %pack_up.1.refs_4_.refs_1_.refs_3_.refs_5_), channel_id=1, source_target_pairs={{0,16},{8,24},{16,0},{24,8},{32,48},{40,56},{48,32},{56,40},{64,80... | collective-permute-start | bytes 1609736 | tf_op jit(solution)/shard_map/ppermute | solution.py:357
  10.5 9.2 %collective-permute-start = (bf16[256,128]{1,0:T(8,128)(2,1)S(1)}, bf16[256,128]{1,0:T(8,128)(2,1)S(1)}, u32[]{:S(2)}, u32[]{:S(2)}) collective-permute-start(bf16[256,128]{1,0:T(8,128)(2,1)S(1)} %rotate.1.refs_0_), channel_id=1, source_target_pairs={{0,192},{8,200},{16,208},{24,216},{32,224},{40,232},{48,240},{56,2... | collective-permute-start | bytes 196616 | tf_op jit(solution)/shard_map/ppermute | solution.py:357
  16.6 5.8 %collective-permute-start.1 = (bf16[256,128]{1,0:T(8,128)(2,1)S(1)}, bf16[256,128]{1,0:T(8,128)(2,1)S(1)}, u32[]{:S(2)}, u32[]{:S(2)}) collective-permute-start(bf16[256,128]{1,0:T(8,128)(2,1)S(1)} %rotate.1.refs_0_), channel_id=1, source_target_pairs={{0,64},{8,72},{16,80},{24,88},{32,96},{40,104},{48,112},{56,120},{... | collective-permute-start | bytes 196616 | tf_op jit(solution)/shard_map/ppermute | solution.py:357
  16.6 5.8 %collective-permute-start.2 = (bf16[256,128]{1,0:T(8,128)(2,1)S(1)}, bf16[256,128]{1,0:T(8,128)(2,1)S(1)}, u32[]{:S(2)}, u32[]{:S(2)}) collective-permute-start(bf16[256,128]{1,0:T(8,128)(2,1)S(1)} %rotate.1.refs_0_), channel_id=1, source_target_pairs={{0,224},{8,232},{16,240},{24,248},{32,0},{40,8},{48,16},{56,24},{6... | collective-permute-start | bytes 196616 | tf_op jit(solution)/shard_map/ppermute | solution.py:357
  19.7 4.8 %collective-permute-start.3 = (bf16[256,128]{1,0:T(8,128)(2,1)S(1)}, bf16[256,128]{1,0:T(8,128)(2,1)S(1)}, u32[]{:S(2)}, u32[]{:S(2)}) collective-permute-start(bf16[256,128]{1,0:T(8,128)(2,1)S(1)} %rotate.1.refs_0_), channel_id=1, source_target_pairs={{0,32},{8,40},{16,48},{24,56},{32,64},{40,72},{48,80},{56,88},{64,... | collective-permute-start | bytes 196616 | tf_op jit(solution)/shard_map/ppermute | solution.py:357
  24.4 6.2 %collective-permute-start.4 = (bf16[2096,128]{1,0:T(8,128)(2,1)S(1)}, bf16[2096,128]{1,0:T(8,128)(2,1)S(1)}, u32[]{:S(2)}, u32[]{:S(2)}) collective-permute-start(bf16[2096,128]{1,0:T(8,128)(2,1)S(1)} %pack_up.1.refs_4_.refs_1_.refs_3_.refs_5_), channel_id=1, source_target_pairs={{0,8},{8,0},{16,24},{24,16},{32,40},{40,32},{48,56},{56,48},{64,72... | collective-permute-start | bytes 1609736 | tf_op jit(solution)/shard_map/ppermute | solution.py:357
  26.3 11.4 %collective-permute-start.6 = (bf16[2096,128]{1,0:T(8,128)(2,1)S(1)}, bf16[2096,128]{1,0:T(8,128)(2,1)S(1)}, u32[]{:S(2)}, u32[]{:S(2)}) collective-permute-start(bf16[2096,128]{1,0:T(8,128)(2,1)S(1)} %collective-permute-done.5.refs_6_.refs_7_.refs_5_), channel_id=1, source_target_pairs={{0,8},{8,0},{16,24},{24,16},{32,40},{40,32},{48,56},{56,48},{64,72... | collective-permute-start | bytes 1609736 | tf_op jit(solution)/shard_map/ppermute | solution.py:357
  26.3 9.0 %collective-permute-start.7 = (bf16[256,128]{1,0:T(8,128)(2,1)S(1)}, bf16[256,128]{1,0:T(8,128)(2,1)S(1)}, u32[]{:S(2)}, u32[]{:S(2)}) collective-permute-start(bf16[256,128]{1,0:T(8,128)(2,1)S(1)} %collective-permute-done.refs_2_.refs_0_), channel_id=1, source_target_pairs={{0,224},{8,232},{16,240},{24,248},{32,0},{40,8},{48,16},{56,24},{6... | collective-permute-start | bytes 196616 | tf_op jit(solution)/shard_map/ppermute | solution.py:357
  29.5 5.8 %collective-permute-start.9 = (bf16[256,128]{1,0:T(8,128)(2,1)S(1)}, bf16[256,128]{1,0:T(8,128)(2,1)S(1)}, u32[]{:S(2)}, u32[]{:S(2)}) collective-permute-start(bf16[256,128]{1,0:T(8,128)(2,1)S(1)} %collective-permute-done.refs_2_.refs_0_), channel_id=1, source_target_pairs={{0,192},{8,200},{16,208},{24,216},{32,224},{40,232},{48,240},{56,2... | collective-permute-start | bytes 196616 | tf_op jit(solution)/shard_map/ppermute | solution.py:357
  30.7 4.6 %collective-permute-start.8 = (bf16[256,128]{1,0:T(8,128)(2,1)S(1)}, bf16[256,128]{1,0:T(8,128)(2,1)S(1)}, u32[]{:S(2)}, u32[]{:S(2)}) collective-permute-start(bf16[256,128]{1,0:T(8,128)(2,1)S(1)} %collective-permute-done.1.refs_3_.refs_1_), channel_id=1, source_target_pairs={{0,32},{8,40},{16,48},{24,56},{32,64},{40,72},{48,80},{56,88},{64,... | collective-permute-start | bytes 196616 | tf_op jit(solution)/shard_map/ppermute | solution.py:357
  40.8 7.5 %collective-permute-start.10 = (bf16[272,128]{1,0:T(8,128)(2,1)S(1)}, bf16[272,128]{1,0:T(8,128)(2,1)S(1)}, u32[]{:S(2)}, u32[]{:S(2)}) collective-permute-start(bf16[272,128]{1,0:T(8,128)(2,1)S(1)} %get-tuple-element.44), channel_id=1, source_target_pairs={{0,32},{8,40},{16,48},{24,56},{32,64},{40,72},{48,80},{56,88},{64,... | collective-permute-start | bytes 208904 | tf_op jit(solution)/shard_map/ppermute | solution.py:357
  41.6 9.4 %collective-permute-start.11 = (bf16[272,128]{1,0:T(8,128)(2,1)S(1)}, bf16[272,128]{1,0:T(8,128)(2,1)S(1)}, u32[]{:S(2)}, u32[]{:S(2)}) collective-permute-start(bf16[272,128]{1,0:T(8,128)(2,1)S(1)} %get-tuple-element.45), channel_id=1, source_target_pairs={{0,64},{8,72},{16,80},{24,88},{32,96},{40,104},{48,112},{56,120},{... | collective-permute-start | bytes 208904 | tf_op jit(solution)/shard_map/ppermute | solution.py:357
  42.2 8.7 %collective-permute-start.12 = (bf16[272,128]{1,0:T(8,128)(2,1)S(1)}, bf16[272,128]{1,0:T(8,128)(2,1)S(1)}, u32[]{:S(2)}, u32[]{:S(2)}) collective-permute-start(bf16[272,128]{1,0:T(8,128)(2,1)S(1)} %get-tuple-element.47), channel_id=1, source_target_pairs={{0,224},{8,232},{16,240},{24,248},{32,0},{40,8},{48,16},{56,24},{6... | collective-permute-start | bytes 208904 | tf_op jit(solution)/shard_map/ppermute | solution.py:357
  48.2 31.5 %copy-start = (bf16[2048,512]{1,0:T(8,128)(2,1)S(1)}, bf16[2048,512]{1,0:T(8,128)(2,1)}, u32[]{:S(2)}) copy-start(bf16[2048,512]{1,0:T(8,128)(2,1)} %refs_8_.1) | copy-start | bytes 6291460
  48.2 8.3 %collective-permute-start.13 = (bf16[272,128]{1,0:T(8,128)(2,1)S(1)}, bf16[272,128]{1,0:T(8,128)(2,1)S(1)}, u32[]{:S(2)}, u32[]{:S(2)}) collective-permute-start(bf16[272,128]{1,0:T(8,128)(2,1)S(1)} %get-tuple-element.36), channel_id=1, source_target_pairs={{0,32},{8,40},{16,48},{24,56},{32,64},{40,72},{48,80},{56,88},{64,... | collective-permute-start | bytes 208904 | tf_op jit(solution)/shard_map/ppermute | solution.py:357
  48.3 8.2 %collective-permute-start.14 = (bf16[272,128]{1,0:T(8,128)(2,1)S(1)}, bf16[272,128]{1,0:T(8,128)(2,1)S(1)}, u32[]{:S(2)}, u32[]{:S(2)}) collective-permute-start(bf16[272,128]{1,0:T(8,128)(2,1)S(1)} %get-tuple-element.51), channel_id=1, source_target_pairs={{0,224},{8,232},{16,240},{24,248},{32,0},{40,8},{48,16},{56,24},{6... | collective-permute-start | bytes 208904 | tf_op jit(solution)/shard_map/ppermute | solution.py:357
  51.4 5.4 %collective-permute-start.15 = (bf16[272,128]{1,0:T(8,128)(2,1)S(1)}, bf16[272,128]{1,0:T(8,128)(2,1)S(1)}, u32[]{:S(2)}, u32[]{:S(2)}) collective-permute-start(bf16[272,128]{1,0:T(8,128)(2,1)S(1)} %get-tuple-element.48), channel_id=1, source_target_pairs={{0,64},{8,72},{16,80},{24,88},{32,96},{40,104},{48,112},{56,120},{... | collective-permute-start | bytes 208904 | tf_op jit(solution)/shard_map/ppermute | solution.py:357
  51.5 6.0 %collective-permute-start.16 = (bf16[272,128]{1,0:T(8,128)(2,1)S(1)}, bf16[272,128]{1,0:T(8,128)(2,1)S(1)}, u32[]{:S(2)}, u32[]{:S(2)}) collective-permute-start(bf16[272,128]{1,0:T(8,128)(2,1)S(1)} %get-tuple-element.52), channel_id=1, source_target_pairs={{0,192},{8,200},{16,208},{24,216},{32,224},{40,232},{48,240},{56,2... | collective-permute-start | bytes 208904 | tf_op jit(solution)/shard_map/ppermute | solution.py:357
  57.7 4.7 %collective-permute-start.17 = (bf16[256,128]{1,0:T(8,128)(2,1)S(1)}, bf16[256,128]{1,0:T(8,128)(2,1)S(1)}, u32[]{:S(2)}, u32[]{:S(2)}) collective-permute-start(bf16[256,128]{1,0:T(8,128)(2,1)S(1)} %merge.3), channel_id=1, source_target_pairs={{0,16},{8,24},{16,0},{24,8},{32,48},{40,56},{48,32},{56,40},{64,80... | collective-permute-start | bytes 196616 | tf_op jit(solution)/shard_map/ppermute | solution.py:357
  62.4 6.4 %collective-permute-start.19 = (bf16[512,128]{1,0:T(8,128)(2,1)S(1)}, bf16[512,128]{1,0:T(8,128)(2,1)S(1)}, u32[]{:S(2)}, u32[]{:S(2)}) collective-permute-start(bf16[512,128]{1,0:T(8,128)(2,1)S(1)} %pad_maximum_fusion.refs_0_), channel_id=1, source_target_pairs={{0,192},{8,200},{16,208},{24,216},{32,224},{40,232},{48,240},{56,2... | collective-permute-start | bytes 393224 | tf_op jit(solution)/shard_map/ppermute | solution.py:357
  65.5 4.7 %collective-permute-start.18 = (bf16[512,128]{1,0:T(8,128)(2,1)S(1)}, bf16[512,128]{1,0:T(8,128)(2,1)S(1)}, u32[]{:S(2)}, u32[]{:S(2)}) collective-permute-start(bf16[512,128]{1,0:T(8,128)(2,1)S(1)} %pad_maximum_fusion.refs_0_), channel_id=1, source_target_pairs={{0,224},{8,232},{16,240},{24,248},{32,0},{40,8},{48,16},{56,24},{6... | collective-permute-start | bytes 393224 | tf_op jit(solution)/shard_map/ppermute | solution.py:357
  65.5 6.6 %collective-permute-start.22 = (bf16[512,128]{1,0:T(8,128)(2,1)S(1)}, bf16[512,128]{1,0:T(8,128)(2,1)S(1)}, u32[]{:S(2)}, u32[]{:S(2)}) collective-permute-start(bf16[512,128]{1,0:T(8,128)(2,1)S(1)} %pad_maximum_fusion.refs_0_), channel_id=1, source_target_pairs={{0,64},{8,72},{16,80},{24,88},{32,96},{40,104},{48,112},{56,120},{... | collective-permute-start | bytes 393224 | tf_op jit(solution)/shard_map/ppermute | solution.py:357
  65.8 8.4 %collective-permute-start.24 = (bf16[512,128]{1,0:T(8,128)(2,1)S(1)}, bf16[512,128]{1,0:T(8,128)(2,1)S(1)}, u32[]{:S(2)}, u32[]{:S(2)}) collective-permute-start(bf16[512,128]{1,0:T(8,128)(2,1)S(1)} %pad_maximum_fusion.refs_0_), channel_id=1, source_target_pairs={{0,32},{8,40},{16,48},{24,56},{32,64},{40,72},{48,80},{56,88},{64,... | collective-permute-start | bytes 393224 | tf_op jit(solution)/shard_map/ppermute | solution.py:357
  68.9 6.5 %collective-permute-start.20 = (bf16[512,128]{1,0:T(8,128)(2,1)S(1)}, bf16[512,128]{1,0:T(8,128)(2,1)S(1)}, u32[]{:S(2)}, u32[]{:S(2)}) collective-permute-start(bf16[512,128]{1,0:T(8,128)(2,1)S(1)} %collective-permute-done.19.refs_2_), channel_id=1, source_target_pairs={{0,224},{8,232},{16,240},{24,248},{32,0},{40,8},{48,16},{56,24},{6... | collective-permute-start | bytes 393224 | tf_op jit(solution)/shard_map/ppermute | solution.py:357
  70.2 8.9 %collective-permute-start.21 = (bf16[512,128]{1,0:T(8,128)(2,1)S(1)}, bf16[512,128]{1,0:T(8,128)(2,1)S(1)}, u32[]{:S(2)}, u32[]{:S(2)}) collective-permute-start(bf16[512,128]{1,0:T(8,128)(2,1)S(1)} %collective-permute-done.19.refs_2_), channel_id=1, source_target_pairs={{0,192},{8,200},{16,208},{24,216},{32,224},{40,232},{48,240},{56,2... | collective-permute-start | bytes 393224 | tf_op jit(solution)/shard_map/ppermute | solution.py:357
  72.1 7.5 %collective-permute-start.23 = (bf16[512,128]{1,0:T(8,128)(2,1)S(1)}, bf16[512,128]{1,0:T(8,128)(2,1)S(1)}, u32[]{:S(2)}, u32[]{:S(2)}) collective-permute-start(bf16[512,128]{1,0:T(8,128)(2,1)S(1)} %collective-permute-done.22.refs_6_), channel_id=1, source_target_pairs={{0,32},{8,40},{16,48},{24,56},{32,64},{40,72},{48,80},{56,88},{64,... | collective-permute-start | bytes 393224 | tf_op jit(solution)/shard_map/ppermute | solution.py:357

commit v2 on v1

--- a/solution.py
+++ b/solution.py
@@ -364,6 +364,8 @@
     )
     cosine, sine = turning(positions, head_width)
     q = {0: rotate(queries, cosine, sine)}
+    for d in (2, -2, 1, -1):
+        q[d] = send(q[0], dz=-d)
     fresh = jnp.concatenate(
         [
             new_keys.reshape(tok_dev, head_width),
@@ -375,22 +377,18 @@
     pack = pack_up(
         cache_keys.reshape(cache_rows, head_width),
         cache_values.reshape(cache_rows, head_width),
-        after(fresh, q[0]),
+        after(fresh, q[2], q[-2]),
         cosine,
         sine,
     )
-    pack_x = send(pack, dx=1)
-    for d in (1, -1, 2, -2):
-        q[d] = send(q[0], dz=-d)
+    pack_x, pack_c = send(pack, dx=1), send(pack, dc=1)
     here, close, wide, outer = (0,), (1, -1), (2, -2), (3, -3, 4)
-    arrived = (q[1], q[-1], q[2], q[-2])
-    pack_c, pack_xc = send(after(pack, *arrived), dc=1), send(after(pack_x, *arrived), dc=1)
-    up, down = after(q[2], *arrived), after(q[-2], *arrived)
-    q[3], q[-3], q[4] = send(up, dz=-1), send(down, dz=1), send(up, dz=-2)
+    q[3], q[-3], q[4] = send(q[2], dz=-1), send(q[-2], dz=1), send(q[2], dz=-2)
     state = {here: flash_first([q[0]], (pack, pack_c))}
     both = flash_first([q[d] for d in close + wide], (pack, pack_c))
     state[close], state[wide] = both, both
-    q[-3] = after(q[-3], both[1], state[here][1])
+    pack_x = after(pack_x, both[1], state[here][1], q[3], q[-3], q[4])
+    pack_xc = send(pack_x, dc=1)
     state[outer] = flash_first([q[d] for d in outer], (pack, pack_c))
     packs = (pack, pack_c, pack_x, pack_xc)
 

time: 104 us -> 103 us (level)
  blocking collectives: 21.2 us -> 18.8 us
  waiting for transfers between devices: 16.3 us -> 17.6 us
    all_to_all x1, blocking collectives: 21.2 us -> 18.8 us  [on_device(): got = lax.all_to_all(terms, ('c', 'kvh'), 0, 0, tiled=True)]
    ppermute x26, waiting for transfers between devices: 16.3 us -> 17.6 us  [send(): return lax.ppermute(value, CTX, permutation(dz, dx, dc))]
  transfers between devices with their start and end apart: 26 -> 26, of which waited for: 12 -> 10; matrix products, arithmetic and copies ran while one was open for 1% -> 1% of each run, Pallas kernels for 16% -> 16%
where the time goes in v2:
time: 103 us; the launch traced here: 102 us
  starting transfers between devices  41.8 us (41%)
  Pallas kernels  18.9 us (18%)
  blocking collectives  18.8 us (18%)
  waiting for transfers between devices  17.6 us (17%)
  local copies, waits for them, and re-layouts  2.82 us (3%)
  between operations  1.51 us (1%)
    ppermute x26, starting transfers between devices, send(): return lax.ppermute(value, CTX, permutation(dz, dx, dc))  41.8 us
    all_to_all x1, blocking collectives, on_device(): got = lax.all_to_all(terms, ('c', 'kvh'), 0, 0, tiled=True)  18.8 us
    ppermute x26, waiting for transfers between devices, send(): return lax.ppermute(value, CTX, permutation(dz, dx, dc))  17.6 us
    pallas_call x4, Pallas kernels, flash_second(): pl.pallas_call(functools.partial(second_kernel, offsets, shards, first),...  8.57 us
    pallas_call x3, Pallas kernels, flash_first(): pl.pallas_call(functools.partial(first_kernel, chunks), out_shape=(jax.Sh...  6.48 us
    unnamed x8, local copies, waits for them, and re-layouts  2.74 us
  transfers between devices with their start and end apart: 26, of which 10 were waited for; matrix products, arithmetic and copies ran while one was open for 1% of the time, Pallas kernels for 16%

profile of v2, /device:TPU:1, one launch (start us, length us, event | category | flops | bytes accessed | tf_op | source)
XLA Modules:
  0.0 102.5 jit_solution(13805147194559758181)
XLA Ops:
  0.0 0.1 compare_select_fusion
  0.8 0.1 fusion
  0.9 0.0 copy-start.3
  0.9 0.8 copy-done.3
  1.7 0.2 rotate.1.refs_0_
  2.0 6.9 %collective-permute-start = (bf16[256,128]{1,0:T(8,128)(2,1)S(1)}, bf16[256,128]{1,0:T(8,128)(2,1)S(1)}, u32[]{:S(2)}, u32[]{:S(2)}) collective-permute-start(bf16[256,128]{1,0:T(8,128)(2,1)S(1)} %rotate.1.refs_0_), channel_id=1, source_target_pairs={{0,192},{8,200},{16,208},{24,216},{32,224},{40,232},{48,240},{56,2... | collective-permute-start | bytes 196616 | tf_op jit(solution)/shard_map/ppermute | solution.py:357
  8.9 0.0 collective-permute-start.1
  8.9 1.0 collective-permute-start.25
  10.5 0.1 pad.4.clone
  10.6 0.8 maximum_maximum_fusion.fresh
  11.4 3.4 %collective-permute-done.1.refs_3_.refs_1_ = bf16[256,128]{1,0:T(8,128)(2,1)S(1)} collective-permute-done((bf16[256,128]{1,0:T(8,128)(2,1)S(1)}, bf16[256,128]{1,0:T(8,128)(2,1)S(1)}, u32[]{:S(2)}, u32[]{:S(2)}) %collective-permute-start.1) | collective-permute-done | bytes 65568 | tf_op jit(solution)/shard_map/ppermute | solution.py:357
  14.8 0.9 copy-done.1
  15.8 0.9 copy-done.2
  16.7 0.8 pack_up.1.refs_4_.refs_1_.refs_3_.refs_5_
  17.5 1.6 %collective-permute-start.4 = (bf16[2096,128]{1,0:T(8,128)(2,1)S(1)}, bf16[2096,128]{1,0:T(8,128)(2,1)S(1)}, u32[]{:S(2)}, u32[]{:S(2)}) collective-permute-start(bf16[2096,128]{1,0:T(8,128)(2,1)S(1)} %pack_up.1.refs_4_.refs_1_.refs_3_.refs_5_), channel_id=1, source_target_pairs={{0,8},{8,0},{16,24},{24,16},{32,40},{40,32},{48,56},{56,48},{64,72... | collective-permute-start | bytes 1609736 | tf_op jit(solution)/shard_map/ppermute | solution.py:357
  19.2 2.8 %collective-permute-start.5 = (bf16[2096,128]{1,0:T(8,128)(2,1)S(1)}, bf16[2096,128]{1,0:T(8,128)(2,1)S(1)}, u32[]{:S(2)}, u32[]{:S(2)}) collective-permute-start(bf16[2096,128]{1,0:T(8,128)(2,1)S(1)} %pack_up.1.refs_4_.refs_1_.refs_3_.refs_5_), channel_id=1, source_target_pairs={{0,16},{8,24},{16,0},{24,8},{32,48},{40,56},{48,32},{56,40},{64,80... | collective-permute-start | bytes 1609736 | tf_op jit(solution)/shard_map/ppermute | solution.py:357
  21.9 1.5 %collective-permute-start.3 = (bf16[256,128]{1,0:T(8,128)(2,1)S(1)}, bf16[256,128]{1,0:T(8,128)(2,1)S(1)}, u32[]{:S(2)}, u32[]{:S(2)}) collective-permute-start(bf16[256,128]{1,0:T(8,128)(2,1)S(1)} %rotate.1.refs_0_), channel_id=1, source_target_pairs={{0,32},{8,40},{16,48},{24,56},{32,64},{40,72},{48,80},{56,88},{64,... | collective-permute-start | bytes 196616 | tf_op jit(solution)/shard_map/ppermute | solution.py:357
  23.4 1.9 %collective-permute-done.2.refs_0_ = bf16[256,128]{1,0:T(8,128)(2,1)S(1)} collective-permute-done((bf16[256,128]{1,0:T(8,128)(2,1)S(1)}, bf16[256,128]{1,0:T(8,128)(2,1)S(1)}, u32[]{:S(2)}, u32[]{:S(2)}) %collective-permute-start.2) | collective-permute-done | bytes 65568 | tf_op jit(solution)/shard_map/ppermute | solution.py:357
  25.4 1.4 %collective-permute-start.6 = (bf16[256,128]{1,0:T(8,128)(2,1)S(1)}, bf16[256,128]{1,0:T(8,128)(2,1)S(1)}, u32[]{:S(2)}, u32[]{:S(2)}) collective-permute-start(bf16[256,128]{1,0:T(8,128)(2,1)S(1)} %collective-permute-done.refs_2_.refs_0_), channel_id=1, source_target_pairs={{0,224},{8,232},{16,240},{24,248},{32,0},{40,8},{48,16},{56,24},{6... | collective-permute-start | bytes 196616 | tf_op jit(solution)/shard_map/ppermute | solution.py:357
  26.8 0.0 collective-permute-start.7
  26.8 0.0 collective-permute-done.4.refs_5_.refs_2_.refs_4_.refs_6_
  26.8 1.2 %collective-permute-start.8 = (bf16[256,128]{1,0:T(8,128)(2,1)S(1)}, bf16[256,128]{1,0:T(8,128)(2,1)S(1)}, u32[]{:S(2)}, u32[]{:S(2)}) collective-permute-start(bf16[256,128]{1,0:T(8,128)(2,1)S(1)} %collective-permute-done.refs_2_.refs_0_), channel_id=1, source_target_pairs={{0,192},{8,200},{16,208},{24,216},{32,224},{40,232},{48,240},{56,2... | collective-permute-start | bytes 196616 | tf_op jit(solution)/shard_map/ppermute | solution.py:357
  28.0 3.0 %flash_first.3 = (f32[4,256,256]{2,1,0:T(8,128)S(1)}, f32[4,256,128]{2,1,0:T(8,128)S(1)}) custom-call(bf16[256,128]{1,0:T(8,128)(2,1)S(1)} %collective-permute-done.2.refs_0_, bf16[256,128]{1,0:T(8,128)(2,1)S(1)} %collective-permute-done.3.refs_1_, bf16[256,128]{1,0:T(8,128)(2,1)S(1)} %collective-permute-done.refs_2_.refs_0_, ...), custom_call_target="tpu_custom_call" | custom-call | flops 2147483648 | bytes 1048576 | tf_op jit(solution)/shard_map/flash_first/pallas_call | solution.py:148
  31.0 1.0 flash_first.4
  32.0 0.0 collective-permute-done.6.refs_0_
  32.0 0.0 collective-permute-done.7.refs_1_
  32.0 2.4 %collective-permute-done.5.refs_6_.refs_7_.refs_5_ = bf16[2096,128]{1,0:T(8,128)(2,1)S(1)} collective-permute-done((bf16[2096,128]{1,0:T(8,128)(2,1)S(1)}, bf16[2096,128]{1,0:T(8,128)(2,1)S(1)}, u32[]{:S(2)}, u32[]{:S(2)}) %collective-permute-start.5) | collective-permute-done | bytes 536608 | tf_op jit(solution)/shard_map/ppermute | solution.py:357
  34.4 0.9 collective-permute-start.9
  35.3 2.5 %flash_first.5 = (f32[3,256,256]{2,1,0:T(8,128)S(1)}, f32[3,256,128]{2,1,0:T(8,128)S(1)}) custom-call(bf16[256,128]{1,0:T(8,128)(2,1)S(1)} %collective-permute-done.6.refs_0_, bf16[256,128]{1,0:T(8,128)(2,1)S(1)} %collective-permute-done.7.refs_1_, bf16[256,128]{1,0:T(8,128)(2,1)S(1)} %collective-permute-done.8.refs_2_, ...), custom_call_target="tpu_custom_call" | custom-call | flops 1610612736 | bytes 1048576 | tf_op jit(solution)/shard_map/flash_first/pallas_call | solution.py:148
  37.8 0.0 collective-permute-done.9.refs_7_.refs_8_.refs_6_
  37.8 3.0 %flash_second.6 = (bf16[272,128]{1,0:T(8,128)(2,1)S(1)}, bf16[272,128]{1,0:T(8,128)(2,1)S(1)}, bf16[272,128]{1,0:T(8,128)(2,1)S(1)}) custom-call(bf16[256,128]{1,0:T(8,128)(2,1)S(1)} %collective-permute-done.6.refs_0_, bf16[256,128]{1,0:T(8,128)(2,1)S(1)} %collective-permute-done.7.refs_1_, bf16[256,128]{1,0:T(8,128)(2,1)S(1)} %collective-permute-done.8.refs_2_, ...), custom_call_target="tpu_custom_call" | custom-call | flops 1048576 | bytes 65536 | tf_op jit(solution)/shard_map/flash_second/pallas_call | solution.py:230
  40.8 1.5 %collective-permute-start.10 = (bf16[272,128]{1,0:T(8,128)(2,1)S(1)}, bf16[272,128]{1,0:T(8,128)(2,1)S(1)}, u32[]{:S(2)}, u32[]{:S(2)}) collective-permute-start(bf16[272,128]{1,0:T(8,128)(2,1)S(1)} %get-tuple-element.36), channel_id=1, source_target_pairs={{0,32},{8,40},{16,48},{24,56},{32,64},{40,72},{48,80},{56,88},{64,... | collective-permute-start | bytes 208904 | tf_op jit(solution)/shard_map/ppermute | solution.py:357
  42.3 0.8 collective-permute-start.11
  43.0 1.7 %collective-permute-start.12 = (bf16[272,128]{1,0:T(8,128)(2,1)S(1)}, bf16[272,128]{1,0:T(8,128)(2,1)S(1)}, u32[]{:S(2)}, u32[]{:S(2)}) collective-permute-start(bf16[272,128]{1,0:T(8,128)(2,1)S(1)} %get-tuple-element.39), channel_id=1, source_target_pairs={{0,224},{8,232},{16,240},{24,248},{32,0},{40,8},{48,16},{56,24},{6... | collective-permute-start | bytes 208904 | tf_op jit(solution)/shard_map/ppermute | solution.py:357
  44.8 2.0 %flash_second.4 = (bf16[272,128]{1,0:T(8,128)(2,1)S(1)}, bf16[272,128]{1,0:T(8,128)(2,1)S(1)}) custom-call(bf16[256,128]{1,0:T(8,128)(2,1)S(1)} %collective-permute-done.refs_2_.refs_0_, bf16[256,128]{1,0:T(8,128)(2,1)S(1)} %collective-permute-done.1.refs_3_.refs_1_, f32[4,256,256]{2,1,0:T(8,128)S(1)} %get-tuple-element.26.refs_2_, ...), custom_call_target="tpu_custom_call" | custom-call | flops 1048576 | bytes 65536 | tf_op jit(solution)/shard_map/flash_second/pallas_call | solution.py:230
  46.8 2.0 %flash_second.5 = (bf16[272,128]{1,0:T(8,128)(2,1)S(1)}, bf16[272,128]{1,0:T(8,128)(2,1)S(1)}) custom-call(bf16[256,128]{1,0:T(8,128)(2,1)S(1)} %collective-permute-done.2.refs_0_, bf16[256,128]{1,0:T(8,128)(2,1)S(1)} %collective-permute-done.3.refs_1_, f32[4,256,256]{2,1,0:T(8,128)S(1)} %get-tuple-element.26.refs_2_, ...), custom_call_target="tpu_custom_call" | custom-call | flops 1048576 | bytes 65536 | tf_op jit(solution)/shard_map/flash_second/pallas_call | solution.py:230
  48.8 0.0 copy-start
  48.8 0.1 collective-permute-start.13
  48.9 0.0 collective-permute-done.10.refs_1_
  48.9 2.7 %collective-permute-start.14 = (bf16[272,128]{1,0:T(8,128)(2,1)S(1)}, bf16[272,128]{1,0:T(8,128)(2,1)S(1)}, u32[]{:S(2)}, u32[]{:S(2)}) collective-permute-start(bf16[272,128]{1,0:T(8,128)(2,1)S(1)} %get-tuple-element.43), channel_id=1, source_target_pairs={{0,224},{8,232},{16,240},{24,248},{32,0},{40,8},{48,16},{56,24},{6... | collective-permute-start | bytes 208904 | tf_op jit(solution)/shard_map/ppermute | solution.py:357
  51.6 0.0 collective-permute-done.11.refs_2_
  51.6 0.0 collective-permute-done.12.refs_4_
  51.6 0.4 merge.2
  52.0 0.1 collective-permute-start.15
  52.1 3.6 %collective-permute-start.16 = (bf16[272,128]{1,0:T(8,128)(2,1)S(1)}, bf16[272,128]{1,0:T(8,128)(2,1)S(1)}, u32[]{:S(2)}, u32[]{:S(2)}) collective-permute-start(bf16[272,128]{1,0:T(8,128)(2,1)S(1)} %get-tuple-element.44), channel_id=1, source_target_pairs={{0,192},{8,200},{16,208},{24,216},{32,224},{40,232},{48,240},{56,2... | collective-permute-start | bytes 208904 | tf_op jit(solution)/shard_map/ppermute | solution.py:357
  55.7 1.5 %flash_second.7.refs_0_ = bf16[272,128]{1,0:T(8,128)(2,1)S(1)} custom-call(bf16[256,128]{1,0:T(8,128)(2,1)S(1)} %rotate.1.refs_0_, f32[1,256,256]{2,1,0:T(8,128)S(1)} %get-tuple-element.42.refs_1_, f32[1,256,128]{2,1,0:T(8,128)S(1)} %get-tuple-element.28.refs_2_, bf16[2096,128]{1,0:T(8,128)(2,1)S(1)} %pack_up.1.refs_4_.refs_1_.refs_3_.refs_5_, ...), custom_call_target="tpu_custom_call" | custom-call | flops 1048576 | bytes 65536 | tf_op jit(solution)/shard_map/flash_second/pallas_call | solution.py:230
  57.2 0.8 collective-permute-done.15.refs_3_
  58.0 0.3 merge.3
  58.3 2.2 %collective-permute-start.17 = (bf16[256,128]{1,0:T(8,128)(2,1)S(1)}, bf16[256,128]{1,0:T(8,128)(2,1)S(1)}, u32[]{:S(2)}, u32[]{:S(2)}) collective-permute-start(bf16[256,128]{1,0:T(8,128)(2,1)S(1)} %merge.3), channel_id=1, source_target_pairs={{0,16},{8,24},{16,0},{24,8},{32,48},{40,56},{48,32},{56,40},{64,80... | collective-permute-start | bytes 196616 | tf_op jit(solution)/shard_map/ppermute | solution.py:357
  60.5 2.5 %collective-permute-done.17 = bf16[256,128]{1,0:T(8,128)(2,1)S(1)} collective-permute-done((bf16[256,128]{1,0:T(8,128)(2,1)S(1)}, bf16[256,128]{1,0:T(8,128)(2,1)S(1)}, u32[]{:S(2)}, u32[]{:S(2)}) %collective-permute-start.17) | collective-permute-done | bytes 65568 | tf_op jit(solution)/shard_map/ppermute | solution.py:357
  63.0 3.9 %collective-permute-start.19 = (bf16[512,128]{1,0:T(8,128)(2,1)S(1)}, bf16[512,128]{1,0:T(8,128)(2,1)S(1)}, u32[]{:S(2)}, u32[]{:S(2)}) collective-permute-start(bf16[512,128]{1,0:T(8,128)(2,1)S(1)} %pad_maximum_fusion.refs_0_), channel_id=1, source_target_pairs={{0,192},{8,200},{16,208},{24,216},{32,224},{40,232},{48,240},{56,2... | collective-permute-start | bytes 393224 | tf_op jit(solution)/shard_map/ppermute | solution.py:357
  66.9 0.2 collective-permute-start.22
  67.2 1.2 %collective-permute-start.24 = (bf16[512,128]{1,0:T(8,128)(2,1)S(1)}, bf16[512,128]{1,0:T(8,128)(2,1)S(1)}, u32[]{:S(2)}, u32[]{:S(2)}) collective-permute-start(bf16[512,128]{1,0:T(8,128)(2,1)S(1)} %pad_maximum_fusion.refs_0_), channel_id=1, source_target_pairs={{0,32},{8,40},{16,48},{24,56},{32,64},{40,72},{48,80},{56,88},{64,... | collective-permute-start | bytes 393224 | tf_op jit(solution)/shard_map/ppermute | solution.py:357
  68.4 1.6 %collective-permute-done.19.refs_2_ = bf16[512,128]{1,0:T(8,128)(2,1)S(1)} collective-permute-done((bf16[512,128]{1,0:T(8,128)(2,1)S(1)}, bf16[512,128]{1,0:T(8,128)(2,1)S(1)}, u32[]{:S(2)}, u32[]{:S(2)}) %collective-permute-start.19) | collective-permute-done | bytes 131104 | tf_op jit(solution)/shard_map/ppermute | solution.py:357
  70.0 1.8 %collective-permute-start.20 = (bf16[512,128]{1,0:T(8,128)(2,1)S(1)}, bf16[512,128]{1,0:T(8,128)(2,1)S(1)}, u32[]{:S(2)}, u32[]{:S(2)}) collective-permute-start(bf16[512,128]{1,0:T(8,128)(2,1)S(1)} %collective-permute-done.19.refs_2_), channel_id=1, source_target_pairs={{0,224},{8,232},{16,240},{24,248},{32,0},{40,8},{48,16},{56,24},{6... | collective-permute-start | bytes 393224 | tf_op jit(solution)/shard_map/ppermute | solution.py:357
  71.8 1.0 collective-permute-done.18.refs_1_
  72.8 1.3 %collective-permute-start.21 = (bf16[512,128]{1,0:T(8,128)(2,1)S(1)}, bf16[512,128]{1,0:T(8,128)(2,1)S(1)}, u32[]{:S(2)}, u32[]{:S(2)}) collective-permute-start(bf16[512,128]{1,0:T(8,128)(2,1)S(1)} %collective-permute-done.19.refs_2_), channel_id=1, source_target_pairs={{0,192},{8,200},{16,208},{24,216},{32,224},{40,232},{48,240},{56,2... | collective-permute-start | bytes 393224 | tf_op jit(solution)/shard_map/ppermute | solution.py:357
  74.1 0.2 collective-permute-done.22.refs_6_
  74.3 3.6 %collective-permute-start.23 = (bf16[512,128]{1,0:T(8,128)(2,1)S(1)}, bf16[512,128]{1,0:T(8,128)(2,1)S(1)}, u32[]{:S(2)}, u32[]{:S(2)}) collective-permute-start(bf16[512,128]{1,0:T(8,128)(2,1)S(1)} %collective-permute-done.22.refs_6_), channel_id=1, source_target_pairs={{0,32},{8,40},{16,48},{24,56},{32,64},{40,72},{48,80},{56,88},{64,... | collective-permute-start | bytes 393224 | tf_op jit(solution)/shard_map/ppermute | solution.py:357
  77.8 1.3 %collective-permute-done.21.refs_4_ = bf16[512,128]{1,0:T(8,128)(2,1)S(1)} collective-permute-done((bf16[512,128]{1,0:T(8,128)(2,1)S(1)}, bf16[512,128]{1,0:T(8,128)(2,1)S(1)}, u32[]{:S(2)}, u32[]{:S(2)}) %collective-permute-start.21) | collective-permute-done | bytes 131104 | tf_op jit(solution)/shard_map/ppermute | solution.py:357
  79.2 2.4 %collective-permute-done.23.refs_5_ = bf16[512,128]{1,0:T(8,128)(2,1)S(1)} collective-permute-done((bf16[512,128]{1,0:T(8,128)(2,1)S(1)}, bf16[512,128]{1,0:T(8,128)(2,1)S(1)}, u32[]{:S(2)}, u32[]{:S(2)}) %collective-permute-start.23) | collective-permute-done | bytes 131104 | tf_op jit(solution)/shard_map/ppermute | solution.py:357
  81.6 1.4 %project.1 = bf16[2,8,32,512]{3,2,1,0:T(8,128)(2,1)S(1)} custom-call(bf16[512,128]{1,0:T(8,128)(2,1)S(1)} %pad_maximum_fusion.refs_0_, bf16[512,128]{1,0:T(8,128)(2,1)S(1)} %collective-permute-done.18.refs_1_, bf16[512,128]{1,0:T(8,128)(2,1)S(1)} %collective-permute-done.19.refs_2_, bf16[512,128]{1,0:T(8,128)(2,1)S(1)} %collective-permute-done.20.refs_3_, ...), custom_call_target="tpu_custom_call" | custom-call | flops 1073741824 | bytes 6291456 | tf_op jit(solution)/shard_map/project/pallas_call | solution.py:302
  83.0 18.8 %all_to_all.5.in_ref = bf16[16,32,512]{2,1,0:T(8,128)(2,1)S(1)} all-to-all(bf16[16,32,512]{2,1,0:T(8,128)(2,1)S(1)} %bitcast.8), channel_id=1, replica_groups=mesh['z'=8,'x'=2,'c'=2,'kvh'=8] {'c','kvh'}, dimensions={0} | all-to-all | bytes 1048576 | tf_op jit(solution)/shard_map/all_to_all | solution.py:423
  101.8 0.7 total.1
  (18 shorter events, 0.1 us)
Async XLA Ops:
  0.9 0.8 copy-start.3
  2.0 9.4 %collective-permute-start = (bf16[256,128]{1,0:T(8,128)(2,1)S(1)}, bf16[256,128]{1,0:T(8,128)(2,1)S(1)}, u32[]{:S(2)}, u32[]{:S(2)}) collective-permute-start(bf16[256,128]{1,0:T(8,128)(2,1)S(1)} %rotate.1.refs_0_), channel_id=1, source_target_pairs={{0,192},{8,200},{16,208},{24,216},{32,224},{40,232},{48,240},{56,2... | collective-permute-start | bytes 196616 | tf_op jit(solution)/shard_map/ppermute | solution.py:357
  8.9 5.9 %collective-permute-start.1 = (bf16[256,128]{1,0:T(8,128)(2,1)S(1)}, bf16[256,128]{1,0:T(8,128)(2,1)S(1)}, u32[]{:S(2)}, u32[]{:S(2)}) collective-permute-start(bf16[256,128]{1,0:T(8,128)(2,1)S(1)} %rotate.1.refs_0_), channel_id=1, source_target_pairs={{0,64},{8,72},{16,80},{24,88},{32,96},{40,104},{48,112},{56,120},{... | collective-permute-start | bytes 196616 | tf_op jit(solution)/shard_map/ppermute | solution.py:357
  8.9 72.7 %collective-permute-start.25 = (bf16[2048,512]{1,0:T(8,128)(2,1)}, bf16[2048,512]{1,0:T(8,128)(2,1)S(1)}, u32[]{:S(2)}, u32[]{:S(2)}) collective-permute-start(bf16[2048,512]{1,0:T(8,128)(2,1)} %refs_8_.1), channel_id=1, source_target_pairs={{0,8},{8,0},{16,24},{24,16},{32,40},{40,32},{48,56},{56,48},{64,72... | collective-permute-start | bytes 6291464 | tf_op jit(solution)/shard_map/ppermute | solution.py:357
  14.8 1.0 copy-start.1
  15.8 0.9 copy-start.2
  17.5 9.3 %collective-permute-start.4 = (bf16[2096,128]{1,0:T(8,128)(2,1)S(1)}, bf16[2096,128]{1,0:T(8,128)(2,1)S(1)}, u32[]{:S(2)}, u32[]{:S(2)}) collective-permute-start(bf16[2096,128]{1,0:T(8,128)(2,1)S(1)} %pack_up.1.refs_4_.refs_1_.refs_3_.refs_5_), channel_id=1, source_target_pairs={{0,8},{8,0},{16,24},{24,16},{32,40},{40,32},{48,56},{56,48},{64,72... | collective-permute-start | bytes 1609736 | tf_op jit(solution)/shard_map/ppermute | solution.py:357
  19.2 15.3 %collective-permute-start.5 = (bf16[2096,128]{1,0:T(8,128)(2,1)S(1)}, bf16[2096,128]{1,0:T(8,128)(2,1)S(1)}, u32[]{:S(2)}, u32[]{:S(2)}) collective-permute-start(bf16[2096,128]{1,0:T(8,128)(2,1)S(1)} %pack_up.1.refs_4_.refs_1_.refs_3_.refs_5_), channel_id=1, source_target_pairs={{0,16},{8,24},{16,0},{24,8},{32,48},{40,56},{48,32},{56,40},{64,80... | collective-permute-start | bytes 1609736 | tf_op jit(solution)/shard_map/ppermute | solution.py:357
  21.9 3.4 %collective-permute-start.2 = (bf16[256,128]{1,0:T(8,128)(2,1)S(1)}, bf16[256,128]{1,0:T(8,128)(2,1)S(1)}, u32[]{:S(2)}, u32[]{:S(2)}) collective-permute-start(bf16[256,128]{1,0:T(8,128)(2,1)S(1)} %rotate.1.refs_0_), channel_id=1, source_target_pairs={{0,224},{8,232},{16,240},{24,248},{32,0},{40,8},{48,16},{56,24},{6... | collective-permute-start | bytes 196616 | tf_op jit(solution)/shard_map/ppermute | solution.py:357
  21.9 4.8 %collective-permute-start.3 = (bf16[256,128]{1,0:T(8,128)(2,1)S(1)}, bf16[256,128]{1,0:T(8,128)(2,1)S(1)}, u32[]{:S(2)}, u32[]{:S(2)}) collective-permute-start(bf16[256,128]{1,0:T(8,128)(2,1)S(1)} %rotate.1.refs_0_), channel_id=1, source_target_pairs={{0,32},{8,40},{16,48},{24,56},{32,64},{40,72},{48,80},{56,88},{64,... | collective-permute-start | bytes 196616 | tf_op jit(solution)/shard_map/ppermute | solution.py:357
  25.4 6.7 %collective-permute-start.6 = (bf16[256,128]{1,0:T(8,128)(2,1)S(1)}, bf16[256,128]{1,0:T(8,128)(2,1)S(1)}, u32[]{:S(2)}, u32[]{:S(2)}) collective-permute-start(bf16[256,128]{1,0:T(8,128)(2,1)S(1)} %collective-permute-done.refs_2_.refs_0_), channel_id=1, source_target_pairs={{0,224},{8,232},{16,240},{24,248},{32,0},{40,8},{48,16},{56,24},{6... | collective-permute-start | bytes 196616 | tf_op jit(solution)/shard_map/ppermute | solution.py:357
  26.8 5.2 %collective-permute-start.7 = (bf16[256,128]{1,0:T(8,128)(2,1)S(1)}, bf16[256,128]{1,0:T(8,128)(2,1)S(1)}, u32[]{:S(2)}, u32[]{:S(2)}) collective-permute-start(bf16[256,128]{1,0:T(8,128)(2,1)S(1)} %collective-permute-done.1.refs_3_.refs_1_), channel_id=1, source_target_pairs={{0,32},{8,40},{16,48},{24,56},{32,64},{40,72},{48,80},{56,88},{64,... | collective-permute-start | bytes 196616 | tf_op jit(solution)/shard_map/ppermute | solution.py:357
  26.8 5.2 %collective-permute-start.8 = (bf16[256,128]{1,0:T(8,128)(2,1)S(1)}, bf16[256,128]{1,0:T(8,128)(2,1)S(1)}, u32[]{:S(2)}, u32[]{:S(2)}) collective-permute-start(bf16[256,128]{1,0:T(8,128)(2,1)S(1)} %collective-permute-done.refs_2_.refs_0_), channel_id=1, source_target_pairs={{0,192},{8,200},{16,208},{24,216},{32,224},{40,232},{48,240},{56,2... | collective-permute-start | bytes 196616 | tf_op jit(solution)/shard_map/ppermute | solution.py:357
  34.4 3.4 %collective-permute-start.9 = (bf16[2096,128]{1,0:T(8,128)(2,1)S(1)}, bf16[2096,128]{1,0:T(8,128)(2,1)S(1)}, u32[]{:S(2)}, u32[]{:S(2)}) collective-permute-start(bf16[2096,128]{1,0:T(8,128)(2,1)S(1)} %collective-permute-done.5.refs_6_.refs_7_.refs_5_), channel_id=1, source_target_pairs={{0,8},{8,0},{16,24},{24,16},{32,40},{40,32},{48,56},{56,48},{64,72... | collective-permute-start | bytes 1609736 | tf_op jit(solution)/shard_map/ppermute | solution.py:357
  40.8 8.1 %collective-permute-start.10 = (bf16[272,128]{1,0:T(8,128)(2,1)S(1)}, bf16[272,128]{1,0:T(8,128)(2,1)S(1)}, u32[]{:S(2)}, u32[]{:S(2)}) collective-permute-start(bf16[272,128]{1,0:T(8,128)(2,1)S(1)} %get-tuple-element.36), channel_id=1, source_target_pairs={{0,32},{8,40},{16,48},{24,56},{32,64},{40,72},{48,80},{56,88},{64,... | collective-permute-start | bytes 208904 | tf_op jit(solution)/shard_map/ppermute | solution.py:357
  42.3 9.3 %collective-permute-start.11 = (bf16[272,128]{1,0:T(8,128)(2,1)S(1)}, bf16[272,128]{1,0:T(8,128)(2,1)S(1)}, u32[]{:S(2)}, u32[]{:S(2)}) collective-permute-start(bf16[272,128]{1,0:T(8,128)(2,1)S(1)} %get-tuple-element.37), channel_id=1, source_target_pairs={{0,64},{8,72},{16,80},{24,88},{32,96},{40,104},{48,112},{56,120},{... | collective-permute-start | bytes 208904 | tf_op jit(solution)/shard_map/ppermute | solution.py:357
  43.0 8.6 %collective-permute-start.12 = (bf16[272,128]{1,0:T(8,128)(2,1)S(1)}, bf16[272,128]{1,0:T(8,128)(2,1)S(1)}, u32[]{:S(2)}, u32[]{:S(2)}) collective-permute-start(bf16[272,128]{1,0:T(8,128)(2,1)S(1)} %get-tuple-element.39), channel_id=1, source_target_pairs={{0,224},{8,232},{16,240},{24,248},{32,0},{40,8},{48,16},{56,24},{6... | collective-permute-start | bytes 208904 | tf_op jit(solution)/shard_map/ppermute | solution.py:357
  48.8 32.7 %copy-start = (bf16[2048,512]{1,0:T(8,128)(2,1)S(1)}, bf16[2048,512]{1,0:T(8,128)(2,1)}, u32[]{:S(2)}) copy-start(bf16[2048,512]{1,0:T(8,128)(2,1)} %refs_8_.1) | copy-start | bytes 6291460
  48.8 8.3 %collective-permute-start.13 = (bf16[272,128]{1,0:T(8,128)(2,1)S(1)}, bf16[272,128]{1,0:T(8,128)(2,1)S(1)}, u32[]{:S(2)}, u32[]{:S(2)}) collective-permute-start(bf16[272,128]{1,0:T(8,128)(2,1)S(1)} %get-tuple-element.32), channel_id=1, source_target_pairs={{0,32},{8,40},{16,48},{24,56},{32,64},{40,72},{48,80},{56,88},{64,... | collective-permute-start | bytes 208904 | tf_op jit(solution)/shard_map/ppermute | solution.py:357
  48.9 8.2 %collective-permute-start.14 = (bf16[272,128]{1,0:T(8,128)(2,1)S(1)}, bf16[272,128]{1,0:T(8,128)(2,1)S(1)}, u32[]{:S(2)}, u32[]{:S(2)}) collective-permute-start(bf16[272,128]{1,0:T(8,128)(2,1)S(1)} %get-tuple-element.43), channel_id=1, source_target_pairs={{0,224},{8,232},{16,240},{24,248},{32,0},{40,8},{48,16},{56,24},{6... | collective-permute-start | bytes 208904 | tf_op jit(solution)/shard_map/ppermute | solution.py:357
  52.0 6.0 %collective-permute-start.15 = (bf16[272,128]{1,0:T(8,128)(2,1)S(1)}, bf16[272,128]{1,0:T(8,128)(2,1)S(1)}, u32[]{:S(2)}, u32[]{:S(2)}) collective-permute-start(bf16[272,128]{1,0:T(8,128)(2,1)S(1)} %get-tuple-element.40), channel_id=1, source_target_pairs={{0,64},{8,72},{16,80},{24,88},{32,96},{40,104},{48,112},{56,120},{... | collective-permute-start | bytes 208904 | tf_op jit(solution)/shard_map/ppermute | solution.py:357
  52.1 5.9 %collective-permute-start.16 = (bf16[272,128]{1,0:T(8,128)(2,1)S(1)}, bf16[272,128]{1,0:T(8,128)(2,1)S(1)}, u32[]{:S(2)}, u32[]{:S(2)}) collective-permute-start(bf16[272,128]{1,0:T(8,128)(2,1)S(1)} %get-tuple-element.44), channel_id=1, source_target_pairs={{0,192},{8,200},{16,208},{24,216},{32,224},{40,232},{48,240},{56,2... | collective-permute-start | bytes 208904 | tf_op jit(solution)/shard_map/ppermute | solution.py:357
  58.3 4.7 %collective-permute-start.17 = (bf16[256,128]{1,0:T(8,128)(2,1)S(1)}, bf16[256,128]{1,0:T(8,128)(2,1)S(1)}, u32[]{:S(2)}, u32[]{:S(2)}) collective-permute-start(bf16[256,128]{1,0:T(8,128)(2,1)S(1)} %merge.3), channel_id=1, source_target_pairs={{0,16},{8,24},{16,0},{24,8},{32,48},{40,56},{48,32},{56,40},{64,80... | collective-permute-start | bytes 196616 | tf_op jit(solution)/shard_map/ppermute | solution.py:357
  63.0 7.0 %collective-permute-start.19 = (bf16[512,128]{1,0:T(8,128)(2,1)S(1)}, bf16[512,128]{1,0:T(8,128)(2,1)S(1)}, u32[]{:S(2)}, u32[]{:S(2)}) collective-permute-start(bf16[512,128]{1,0:T(8,128)(2,1)S(1)} %pad_maximum_fusion.refs_0_), channel_id=1, source_target_pairs={{0,192},{8,200},{16,208},{24,216},{32,224},{40,232},{48,240},{56,2... | collective-permute-start | bytes 393224 | tf_op jit(solution)/shard_map/ppermute | solution.py:357
  66.9 5.8 %collective-permute-start.18 = (bf16[512,128]{1,0:T(8,128)(2,1)S(1)}, bf16[512,128]{1,0:T(8,128)(2,1)S(1)}, u32[]{:S(2)}, u32[]{:S(2)}) collective-permute-start(bf16[512,128]{1,0:T(8,128)(2,1)S(1)} %pad_maximum_fusion.refs_0_), channel_id=1, source_target_pairs={{0,224},{8,232},{16,240},{24,248},{32,0},{40,8},{48,16},{56,24},{6... | collective-permute-start | bytes 393224 | tf_op jit(solution)/shard_map/ppermute | solution.py:357
  66.9 7.3 %collective-permute-start.22 = (bf16[512,128]{1,0:T(8,128)(2,1)S(1)}, bf16[512,128]{1,0:T(8,128)(2,1)S(1)}, u32[]{:S(2)}, u32[]{:S(2)}) collective-permute-start(bf16[512,128]{1,0:T(8,128)(2,1)S(1)} %pad_maximum_fusion.refs_0_), channel_id=1, source_target_pairs={{0,64},{8,72},{16,80},{24,88},{32,96},{40,104},{48,112},{56,120},{... | collective-permute-start | bytes 393224 | tf_op jit(solution)/shard_map/ppermute | solution.py:357
  67.2 10.7 %collective-permute-start.24 = (bf16[512,128]{1,0:T(8,128)(2,1)S(1)}, bf16[512,128]{1,0:T(8,128)(2,1)S(1)}, u32[]{:S(2)}, u32[]{:S(2)}) collective-permute-start(bf16[512,128]{1,0:T(8,128)(2,1)S(1)} %pad_maximum_fusion.refs_0_), channel_id=1, source_target_pairs={{0,32},{8,40},{16,48},{24,56},{32,64},{40,72},{48,80},{56,88},{64,... | collective-permute-start | bytes 393224 | tf_op jit(solution)/shard_map/ppermute | solution.py:357
  70.0 7.8 %collective-permute-start.20 = (bf16[512,128]{1,0:T(8,128)(2,1)S(1)}, bf16[512,128]{1,0:T(8,128)(2,1)S(1)}, u32[]{:S(2)}, u32[]{:S(2)}) collective-permute-start(bf16[512,128]{1,0:T(8,128)(2,1)S(1)} %collective-permute-done.19.refs_2_), channel_id=1, source_target_pairs={{0,224},{8,232},{16,240},{24,248},{32,0},{40,8},{48,16},{56,24},{6... | collective-permute-start | bytes 393224 | tf_op jit(solution)/shard_map/ppermute | solution.py:357
  72.8 6.4 %collective-permute-start.21 = (bf16[512,128]{1,0:T(8,128)(2,1)S(1)}, bf16[512,128]{1,0:T(8,128)(2,1)S(1)}, u32[]{:S(2)}, u32[]{:S(2)}) collective-permute-start(bf16[512,128]{1,0:T(8,128)(2,1)S(1)} %collective-permute-done.19.refs_2_), channel_id=1, source_target_pairs={{0,192},{8,200},{16,208},{24,216},{32,224},{40,232},{48,240},{56,2... | collective-permute-start | bytes 393224 | tf_op jit(solution)/shard_map/ppermute | solution.py:357
  74.3 7.3 %collective-permute-start.23 = (bf16[512,128]{1,0:T(8,128)(2,1)S(1)}, bf16[512,128]{1,0:T(8,128)(2,1)S(1)}, u32[]{:S(2)}, u32[]{:S(2)}) collective-permute-start(bf16[512,128]{1,0:T(8,128)(2,1)S(1)} %collective-permute-done.22.refs_6_), channel_id=1, source_target_pairs={{0,32},{8,40},{16,48},{24,56},{32,64},{40,72},{48,80},{56,88},{64,... | collective-permute-start | bytes 393224 | tf_op jit(solution)/shard_map/ppermute | solution.py:357
